TPU v7x, 512 devices: a whole 4x4x16 slice. The times are simulated.
512 devices in a mesh: ctx: 16 (over z), head: 8 (over y, x_hi), section: 4 (over x_lo, core).
Axes of the slice: x: 4 (x_hi: 2, x_lo: 2; x = x_hi * 2 + x_lo), y: 4, z: 16, core: 2. Of those that a mesh axis runs over, the one named last changes fastest.
Arguments:
- query_rows: bfloat16 [4, 4096, 3072], P('section', ('ctx', 'head')), may hold values from -6 to 6
- key_rows: bfloat16 [4, 4096, 1024], P('section', ('ctx', 'head')), may hold values from -6 to 6
- value_rows: bfloat16 [4, 4096, 1024], P('section', ('ctx', 'head')), may hold values from -6 to 6
- grad_out: bfloat16 [4, 4096, 3072], P('section', ('ctx', 'head')), may hold values from -6 to 6
- log_sum_exp: float32 [4, 24, 4096], P('section', None, ('ctx', 'head')), may hold values from 2 to 5
- delta_rows: float32 [4, 24, 4096], P('section', None, ('ctx', 'head')), may hold values from -16 to 16
- doc_lengths: int32 [4, 4], P('section'), may hold values from 1 to 2048, 4096 in all within a row
- block_map: int32 [16, 2], replicated, may hold values from 0 to 31, as said below
Outputs:
- grad_query: bfloat16 [4, 4096, 3072], P('section', ('ctx', 'head'))
- grad_key: bfloat16 [4, 4096, 1024], P('section', ('ctx', 'head'))
- grad_value: bfloat16 [4, 4096, 1024], P('section', ('ctx', 'head'))
Inputs may be any that keep to these rules, and one draw needn't show every extreme that they name: Index i of ctx holds the sequence blocks block_map[i, 0] and block_map[i, 1] = 31 - block_map[i, 0]; column 0 holds each of 0 to 15 once. `doc_lengths`: each row sums to 4096; its longest document has exactly 2048 tokens.
All inputs are finite; a program needn't handle non-finite values.
Results may differ from a plain program's by a relative error of at most 0.013.
Values may be sent and summed in bfloat16 or wider, within the bound.
A program may use at most 64 MiB of HBM per device.

v0:
```python
import jax
import jax.numpy as jnp
from jax import lax
from jax.sharding import PartitionSpec as P

D_HEAD = 128


def shifted(block, axis, distance):
    devices = range(lax.axis_size(axis))
    route = [((i - distance) % len(devices), i) for i in devices]
    return lax.ppermute(block, axis, route)


def token_places(block_map, source, row_count):
    half_rows = row_count // 2
    offsets = jnp.arange(row_count, dtype=jnp.int32)
    block_pair = lax.dynamic_index_in_dim(block_map, source, 0, keepdims=False)
    first_start = block_pair[0] * half_rows
    second_start = block_pair[1] * half_rows - half_rows
    return jnp.where(offsets < half_rows, first_start + offsets, second_start + offsets)


def doc_labels(places, doc_ends):
    return jnp.sum((doc_ends[None, :] <= places[:, None]).astype(jnp.int32), axis=1)


def pair_mask(query_places, query_docs, key_places, key_docs):
    return (query_docs[:, None] == key_docs[None, :]) & (
        key_places[None, :] <= query_places[:, None]
    )


def block_terms(
    query_part, grad_part, lse_part, delta_part, key_part, value_part, allowed, score_scale
):
    query_count = query_part.shape[0]
    key_count = key_part.shape[0]
    shared_heads = key_part.shape[1] // D_HEAD
    group_size = query_part.shape[1] // key_part.shape[1]
    query_heads = query_part.reshape(query_count, shared_heads, group_size, D_HEAD)
    grad_heads = grad_part.reshape(query_count, shared_heads, group_size, D_HEAD)
    key_heads = key_part.reshape(key_count, shared_heads, D_HEAD)
    value_heads = value_part.reshape(key_count, shared_heads, D_HEAD)
    lse_heads = lse_part.reshape(shared_heads, group_size, query_count)
    delta_heads = delta_part.reshape(shared_heads, group_size, query_count)
    scores = jnp.einsum(
        "ikgd,jkd->kgij", query_heads, key_heads, preferred_element_type=jnp.float32
    )
    weights = jnp.where(allowed, jnp.exp(scores * score_scale - lse_heads[..., None]), 0.0)
    weights_half = weights.astype(jnp.bfloat16)
    grad_prob = jnp.einsum(
        "ikgd,jkd->kgij", grad_heads, value_heads, preferred_element_type=jnp.float32
    )
    dscore = (weights * (grad_prob - delta_heads[..., None])).astype(jnp.bfloat16)
    value_terms = jnp.einsum(
        "kgij,ikgd->jkd", weights_half, grad_heads, preferred_element_type=jnp.float32
    )
    key_terms = jnp.einsum(
        "kgij,ikgd->jkd", dscore, query_heads, preferred_element_type=jnp.float32
    )
    query_terms = jnp.einsum(
        "kgij,jkd->ikgd", dscore, key_heads, preferred_element_type=jnp.float32
    )
    return (
        query_terms.reshape(query_count, -1),
        key_terms.reshape(key_count, -1),
        value_terms.reshape(key_count, -1),
    )


def body(
    query_rows, key_rows, value_rows, grad_out, log_sum_exp, delta_rows, doc_lengths, block_map
):
    query_local, grad_local, key_local, value_local = (
        lax.all_to_all(query_rows, "head", split_axis=2, concat_axis=1, tiled=True),
        lax.all_to_all(grad_out, "head", split_axis=2, concat_axis=1, tiled=True),
        lax.all_to_all(key_rows, "head", split_axis=2, concat_axis=1, tiled=True),
        lax.all_to_all(value_rows, "head", split_axis=2, concat_axis=1, tiled=True),
    )
    lse_local, delta_local = (
        lax.all_to_all(log_sum_exp, "head", split_axis=1, concat_axis=2, tiled=True),
        lax.all_to_all(delta_rows, "head", split_axis=1, concat_axis=2, tiled=True),
    )
    query_local = query_local[0]
    grad_local = grad_local[0]
    key_local = key_local[0]
    value_local = value_local[0]
    lse_local = lse_local[0]
    delta_local = delta_local[0]
    ctx_size = lax.axis_size("ctx")
    own_index = lax.axis_index("ctx")
    row_count = query_local.shape[0]
    score_scale = D_HEAD ** (-0.5)
    doc_ends = jnp.cumsum(doc_lengths[0])
    own_places = token_places(block_map, own_index, row_count)
    own_docs = doc_labels(own_places, doc_ends)
    zero_query = jnp.zeros(query_local.shape, jnp.float32)
    zero_keys = jnp.zeros(key_local.shape, jnp.float32)

    def visitor(turn_index):
        source = (own_index - turn_index) % ctx_size
        places = token_places(block_map, source, row_count)
        return (places, doc_labels(places, doc_ends))

    def visit_queries(turn_index, moving, query_total, key_total, value_total):
        places, documents = visitor(turn_index)
        allowed = pair_mask(places, documents, own_places, own_docs)
        terms = block_terms(
            moving[0], moving[1], moving[2], moving[3], key_local, value_local, allowed, score_scale
        )
        return (query_total + terms[0], key_total + terms[1], value_total + terms[2])

    first_totals = visit_queries(
        0, (query_local, grad_local, lse_local, delta_local), zero_query, zero_keys, zero_keys
    )

    def query_turn(turn_index, loop_state):
        moving_query, moving_grad, moving_lse, moving_delta, query_total, key_total, value_total = (
            loop_state
        )
        moving_query, moving_grad = shifted((moving_query, moving_grad), "ctx", 1)
        moving_lse, moving_delta = shifted((moving_lse, moving_delta), "ctx", 1)
        query_total = shifted(query_total, "ctx", 1)
        query_total, key_total, value_total = visit_queries(
            turn_index,
            (moving_query, moving_grad, moving_lse, moving_delta),
            query_total,
            key_total,
            value_total,
        )
        return (
            moving_query,
            moving_grad,
            moving_lse,
            moving_delta,
            query_total,
            key_total,
            value_total,
        )

    loop_state = lax.fori_loop(
        1, ctx_size, query_turn, (query_local, grad_local, lse_local, delta_local) + first_totals
    )
    query_total = shifted(loop_state[4].astype(jnp.bfloat16), "ctx", 1).astype(jnp.float32)
    key_total = loop_state[5]
    value_total = loop_state[6]
    grad_query = (query_total * score_scale).astype(jnp.bfloat16)[None]
    grad_key = (key_total * score_scale).astype(jnp.bfloat16)[None]
    grad_value = value_total.astype(jnp.bfloat16)[None]
    token_query, token_key, token_value = (
        lax.all_to_all(grad_query, "head", split_axis=1, concat_axis=2, tiled=True),
        lax.all_to_all(grad_key, "head", split_axis=1, concat_axis=2, tiled=True),
        lax.all_to_all(grad_value, "head", split_axis=1, concat_axis=2, tiled=True),
    )
    sent_query, sent_key, sent_value = shifted((token_query, token_key, token_value), "section", -1)
    return (sent_query, sent_key, sent_value)


def solution(mesh):
    return jax.shard_map(
        body,
        mesh=mesh,
        in_specs=(
            P("section", ("ctx", "head"), None),
            P("section", ("ctx", "head"), None),
            P("section", ("ctx", "head"), None),
            P("section", ("ctx", "head"), None),
            P("section", None, ("ctx", "head")),
            P("section", None, ("ctx", "head")),
            P("section", None),
            P(),
        ),
        out_specs=(
            P("section", ("ctx", "head"), None),
            P("section", ("ctx", "head"), None),
            P("section", ("ctx", "head"), None),
        ),
        check_vma=False,
    )
```

profile of v0, /device:TPU:1, one launch (start us, length us, event | category | flops | bytes accessed | tf_op | source)
XLA Modules:
  0.0 560.1 jit_solution(4310404991360682364)
XLA Ops:
  0.6 7.6 %all-to-all-start.2 = ((f32[1,24,32]{2,0,1:T(1,128)}), f32[1,24,32]{2,0,1:T(1,128)S(1)}, u32[]{:S(2)}, u32[]{:S(2)}) async-start(f32[1,24,32]{2,0,1:T(1,128)} %bitcast.302), calls=%async_computation.2 | async-start | bytes 24576 | tf_op jit(solution)/shard_map/all_to_all | solution.py:82
  33.3 17.0 %reduce = bf16[3072,32]{1,0:T(8,128)(2,1)S(1)} reduce(bf16[3072,1,32]{2,1,0:T(2,128)(2,1)S(1)} %bitcast.264, bf16[]{:T(256)} %broadcast.119), dimensions={1}, to_apply=%bitcast.181.reduce_sub_computation | reduce | bytes 393218
  53.6 17.2 %reduce.1 = bf16[3072,32]{1,0:T(8,128)(2,1)S(1)} reduce(bf16[3072,1,32]{2,1,0:T(2,128)(2,1)S(1)} %bitcast.265, bf16[]{:T(256)} %broadcast.119), dimensions={1}, to_apply=%bitcast.183.reduce_sub_computation | reduce | bytes 393218
  75.9 6.6 %all-to-all-start.5 = ((bf16[8,2,2048]{2,1,0:T(2,128)(2,1)}), bf16[8,2,2048]{2,1,0:T(2,128)(2,1)S(1)}, u32[]{:S(2)}, u32[]{:S(2)}) async-start(bf16[8,2,2048]{2,1,0:T(2,128)(2,1)} %reshape.320), calls=%async_computation.5 | async-start | bytes 131072 | tf_op jit(solution)/shard_map/all_to_all | solution.py:79
  83.2 6.0 %all-to-all-done.5 = bf16[8,2,2048]{2,1,0:T(2,128)(2,1)S(1)} async-done(((bf16[8,2,2048]{2,1,0:T(2,128)(2,1)}), bf16[8,2,2048]{2,1,0:T(2,128)(2,1)S(1)}, u32[]{:S(2)}, u32[]{:S(2)}) %all-to-all-start.5) | async-done | bytes 65568 | tf_op jit(solution)/shard_map/all_to_all | solution.py:79
  93.4 6.4 %all-to-all-done = bf16[8,2,6144]{2,1,0:T(2,128)(2,1)S(1)} async-done(((bf16[8,2,6144]{2,1,0:T(2,128)(2,1)}), bf16[8,2,6144]{2,1,0:T(2,128)(2,1)S(1)}, u32[]{:S(2)}, u32[]{:S(2)}) %all-to-all-start) | async-done | bytes 196640 | tf_op jit(solution)/shard_map/all_to_all | solution.py:76
  114.7 371.4 %while.28 = (s32[]{:T(128)}, bf16[256,384]{0,1:T(8,128)(2,1)S(1)}, bf16[256,384]{0,1:T(8,128)(2,1)S(1)}, f32[3,256]{1,0:T(4,128)S(1)}, f32[3,256]{1,0:T(4,128)S(...) while((s32[]{:T(128)}, bf16[256,384]{0,1:T(8,128)(2,1)S(1)}, ...), condition=%wide.region_5.6_spmd.clone, body=%wide.region_3.5_spmd.clone.sunk | while | flops 253399824 | bytes 10734224 | solution.py:142
  185.8 8.1 %collective-permute-done.4 = f32[256,384]{0,1:T(8,128)S(1)} collective-permute-done((f32[256,384]{0,1:T(8,128)S(1)}, f32[256,384]{0,1:T(8,128)S(1)}, u32[]{:S(2)}, u32[]{:S(2)}) %collective-permute-start.4) | collective-permute-done | bytes 393248 | tf_op jit(solution)/shard_map/while/body/eval_jaxpr/ppermute | solution.py:12
  208.2 6.8 %collective-permute-done.4 = f32[256,384]{0,1:T(8,128)S(1)} collective-permute-done((f32[256,384]{0,1:T(8,128)S(1)}, f32[256,384]{0,1:T(8,128)S(1)}, u32[]{:S(2)}, u32[]{:S(2)}) %collective-permute-start.4) | collective-permute-done | bytes 393248 | tf_op jit(solution)/shard_map/while/body/eval_jaxpr/ppermute | solution.py:12
  262.2 5.9 %collective-permute-start.1 = (bf16[256,384]{0,1:T(8,128)(2,1)S(1)}, bf16[256,384]{0,1:T(8,128)(2,1)S(1)}, u32[]{:S(2)}, u32[]{:S(2)}) collective-permute-start(bf16[256,384]{0,1:T(8,128)(2,1)S(1)} %get-tuple-element.679), channel_id=1, source_target_pairs={{480,0},{0,32},{32,64},{64,96},{96,128},{128,160},{160,192},{192,2... | collective-permute-start | bytes 589832 | tf_op jit(solution)/shard_map/while/body/eval_jaxpr/ppermute | solution.py:12
  282.0 7.3 %collective-permute-done.4 = f32[256,384]{0,1:T(8,128)S(1)} collective-permute-done((f32[256,384]{0,1:T(8,128)S(1)}, f32[256,384]{0,1:T(8,128)S(1)}, u32[]{:S(2)}, u32[]{:S(2)}) %collective-permute-start.4) | collective-permute-done | bytes 393248 | tf_op jit(solution)/shard_map/while/body/eval_jaxpr/ppermute | solution.py:12
  321.0 8.6 %collective-permute-done.4 = f32[256,384]{0,1:T(8,128)S(1)} collective-permute-done((f32[256,384]{0,1:T(8,128)S(1)}, f32[256,384]{0,1:T(8,128)S(1)}, u32[]{:S(2)}, u32[]{:S(2)}) %collective-permute-start.4) | collective-permute-done | bytes 393248 | tf_op jit(solution)/shard_map/while/body/eval_jaxpr/ppermute | solution.py:12
  346.8 5.8 %collective-permute-done.4 = f32[256,384]{0,1:T(8,128)S(1)} collective-permute-done((f32[256,384]{0,1:T(8,128)S(1)}, f32[256,384]{0,1:T(8,128)S(1)}, u32[]{:S(2)}, u32[]{:S(2)}) %collective-permute-start.4) | collective-permute-done | bytes 393248 | tf_op jit(solution)/shard_map/while/body/eval_jaxpr/ppermute | solution.py:12
  356.1 7.2 %collective-permute-start.1 = (bf16[256,384]{0,1:T(8,128)(2,1)S(1)}, bf16[256,384]{0,1:T(8,128)(2,1)S(1)}, u32[]{:S(2)}, u32[]{:S(2)}) collective-permute-start(bf16[256,384]{0,1:T(8,128)(2,1)S(1)} %get-tuple-element.679), channel_id=1, source_target_pairs={{480,0},{0,32},{32,64},{64,96},{96,128},{128,160},{160,192},{192,2... | collective-permute-start | bytes 589832 | tf_op jit(solution)/shard_map/while/body/eval_jaxpr/ppermute | solution.py:12
  379.1 8.1 %collective-permute-done.4 = f32[256,384]{0,1:T(8,128)S(1)} collective-permute-done((f32[256,384]{0,1:T(8,128)S(1)}, f32[256,384]{0,1:T(8,128)S(1)}, u32[]{:S(2)}, u32[]{:S(2)}) %collective-permute-start.4) | collective-permute-done | bytes 393248 | tf_op jit(solution)/shard_map/while/body/eval_jaxpr/ppermute | solution.py:12
  400.6 6.3 %collective-permute-done.4 = f32[256,384]{0,1:T(8,128)S(1)} collective-permute-done((f32[256,384]{0,1:T(8,128)S(1)}, f32[256,384]{0,1:T(8,128)S(1)}, u32[]{:S(2)}, u32[]{:S(2)}) %collective-permute-start.4) | collective-permute-done | bytes 393248 | tf_op jit(solution)/shard_map/while/body/eval_jaxpr/ppermute | solution.py:12
  434.4 6.0 %collective-permute-start.4 = (f32[256,384]{0,1:T(8,128)S(1)}, f32[256,384]{0,1:T(8,128)S(1)}, u32[]{:S(2)}, u32[]{:S(2)}) collective-permute-start(f32[256,384]{0,1:T(8,128)S(1)} %get-tuple-element.682), channel_id=1, source_target_pairs={{480,0},{0,32},{32,64},{64,96},{96,128},{128,160},{160,192},{192,2... | collective-permute-start | bytes 1179656 | tf_op jit(solution)/shard_map/while/body/eval_jaxpr/ppermute | solution.py:12
  447.2 6.5 %collective-permute-start = (bf16[256,384]{0,1:T(8,128)(2,1)S(1)}, bf16[256,384]{0,1:T(8,128)(2,1)S(1)}, u32[]{:S(2)}, u32[]{:S(2)}) collective-permute-start(bf16[256,384]{0,1:T(8,128)(2,1)S(1)} %get-tuple-element.678), channel_id=1, source_target_pairs={{480,0},{0,32},{32,64},{64,96},{96,128},{128,160},{160,192},{192,2... | collective-permute-start | bytes 589832 | tf_op jit(solution)/shard_map/while/body/eval_jaxpr/ppermute | solution.py:12
  453.8 5.8 %collective-permute-start.1 = (bf16[256,384]{0,1:T(8,128)(2,1)S(1)}, bf16[256,384]{0,1:T(8,128)(2,1)S(1)}, u32[]{:S(2)}, u32[]{:S(2)}) collective-permute-start(bf16[256,384]{0,1:T(8,128)(2,1)S(1)} %get-tuple-element.679), channel_id=1, source_target_pairs={{480,0},{0,32},{32,64},{64,96},{96,128},{128,160},{160,192},{192,2... | collective-permute-start | bytes 589832 | tf_op jit(solution)/shard_map/while/body/eval_jaxpr/ppermute | solution.py:12
  459.6 8.5 %collective-permute-start.2 = (f32[3,256]{1,0:T(4,128)S(1)}, f32[3,256]{1,0:T(4,128)S(1)}, u32[]{:S(2)}, u32[]{:S(2)}) collective-permute-start(f32[3,256]{1,0:T(4,128)S(1)} %get-tuple-element.680), channel_id=1, source_target_pairs={{480,0},{0,32},{32,64},{64,96},{96,128},{128,160},{160,192},{192,2... | collective-permute-start | bytes 9224 | tf_op jit(solution)/shard_map/while/body/eval_jaxpr/ppermute | solution.py:12
  479.1 7.0 %collective-permute-done.4 = f32[256,384]{0,1:T(8,128)S(1)} collective-permute-done((f32[256,384]{0,1:T(8,128)S(1)}, f32[256,384]{0,1:T(8,128)S(1)}, u32[]{:S(2)}, u32[]{:S(2)}) %collective-permute-start.4) | collective-permute-done | bytes 393248 | tf_op jit(solution)/shard_map/while/body/eval_jaxpr/ppermute | solution.py:12
  488.2 5.7 %collective-permute-done.5 = bf16[256,384]{1,0:T(8,128)(2,1)S(1)} collective-permute-done((bf16[256,384]{1,0:T(8,128)(2,1)S(1)}, bf16[256,384]{1,0:T(8,128)(2,1)S(1)}, u32[]{:S(2)}, u32[]{:S(2)}) %collective-permute-start.5) | collective-permute-done | bytes 196640 | tf_op jit(solution)/shard_map/ppermute | solution.py:12
  511.0 26.1 %collective-permute-start.6 = (bf16[1,32,3072]{2,1,0:T(8,128)(2,1)S(1)}, bf16[1,32,3072]{2,1,0:T(8,128)(2,1)S(1)}, u32[]{:S(2)}, u32[]{:S(2)}) collective-permute-start(bf16[1,32,3072]{2,1,0:T(8,128)(2,1)S(1)} %bitcast.295), channel_id=1, source_target_pairs={{1,0},{2,1},{3,2},{0,3},{5,4},{6,5},{7,6},{4,7},{9,8},{10,9},{11,1... | collective-permute-start | bytes 589832 | tf_op jit(solution)/shard_map/ppermute | solution.py:12
  538.9 6.9 %all-to-all-start.8 = ((bf16[8,2,2048]{2,1,0:T(2,128)(2,1)}), bf16[8,2,2048]{2,1,0:T(2,128)(2,1)S(1)}, u32[]{:S(2)}, u32[]{:S(2)}) async-start(bf16[8,2,2048]{2,1,0:T(2,128)(2,1)} %reshape.326), calls=%async_computation.8 | async-start | bytes 131072 | tf_op jit(solution)/shard_map/all_to_all | solution.py:154
  (480 shorter events, 336.6 us)
Async XLA Ops:
  0.6 14.2 %all-to-all-start.2 = ((f32[1,24,32]{2,0,1:T(1,128)}), f32[1,24,32]{2,0,1:T(1,128)S(1)}, u32[]{:S(2)}, u32[]{:S(2)}) async-start(f32[1,24,32]{2,0,1:T(1,128)} %bitcast.302), calls=%async_computation.2 | async-start | bytes 24576 | tf_op jit(solution)/shard_map/all_to_all | solution.py:82
  26.3 49.6 %all-to-all-start.4 = ((bf16[8,2,2048]{2,1,0:T(2,128)(2,1)}), bf16[8,2,2048]{2,1,0:T(2,128)(2,1)S(1)}, u32[]{:S(2)}, u32[]{:S(2)}) async-start(bf16[8,2,2048]{2,1,0:T(2,128)(2,1)} %reshape.318), calls=%async_computation.4 | async-start | bytes 131072 | tf_op jit(solution)/shard_map/all_to_all | solution.py:78
  114.7 21.2 %collective-permute-start = (bf16[256,384]{0,1:T(8,128)(2,1)S(1)}, bf16[256,384]{0,1:T(8,128)(2,1)S(1)}, u32[]{:S(2)}, u32[]{:S(2)}) collective-permute-start(bf16[256,384]{0,1:T(8,128)(2,1)S(1)} %get-tuple-element.678), channel_id=1, source_target_pairs={{480,0},{0,32},{32,64},{64,96},{96,128},{128,160},{160,192},{192,2... | collective-permute-start | bytes 589832 | tf_op jit(solution)/shard_map/while/body/eval_jaxpr/ppermute | solution.py:12
  118.2 18.0 %collective-permute-start.1 = (bf16[256,384]{0,1:T(8,128)(2,1)S(1)}, bf16[256,384]{0,1:T(8,128)(2,1)S(1)}, u32[]{:S(2)}, u32[]{:S(2)}) collective-permute-start(bf16[256,384]{0,1:T(8,128)(2,1)S(1)} %get-tuple-element.679), channel_id=1, source_target_pairs={{480,0},{0,32},{32,64},{64,96},{96,128},{128,160},{160,192},{192,2... | collective-permute-start | bytes 589832 | tf_op jit(solution)/shard_map/while/body/eval_jaxpr/ppermute | solution.py:12
  141.6 17.9 %collective-permute-start = (bf16[256,384]{0,1:T(8,128)(2,1)S(1)}, bf16[256,384]{0,1:T(8,128)(2,1)S(1)}, u32[]{:S(2)}, u32[]{:S(2)}) collective-permute-start(bf16[256,384]{0,1:T(8,128)(2,1)S(1)} %get-tuple-element.678), channel_id=1, source_target_pairs={{480,0},{0,32},{32,64},{64,96},{96,128},{128,160},{160,192},{192,2... | collective-permute-start | bytes 589832 | tf_op jit(solution)/shard_map/while/body/eval_jaxpr/ppermute | solution.py:12
  143.5 16.4 %collective-permute-start.1 = (bf16[256,384]{0,1:T(8,128)(2,1)S(1)}, bf16[256,384]{0,1:T(8,128)(2,1)S(1)}, u32[]{:S(2)}, u32[]{:S(2)}) collective-permute-start(bf16[256,384]{0,1:T(8,128)(2,1)S(1)} %get-tuple-element.679), channel_id=1, source_target_pairs={{480,0},{0,32},{32,64},{64,96},{96,128},{128,160},{160,192},{192,2... | collective-permute-start | bytes 589832 | tf_op jit(solution)/shard_map/while/body/eval_jaxpr/ppermute | solution.py:12
  165.6 18.7 %collective-permute-start = (bf16[256,384]{0,1:T(8,128)(2,1)S(1)}, bf16[256,384]{0,1:T(8,128)(2,1)S(1)}, u32[]{:S(2)}, u32[]{:S(2)}) collective-permute-start(bf16[256,384]{0,1:T(8,128)(2,1)S(1)} %get-tuple-element.678), channel_id=1, source_target_pairs={{480,0},{0,32},{32,64},{64,96},{96,128},{128,160},{160,192},{192,2... | collective-permute-start | bytes 589832 | tf_op jit(solution)/shard_map/while/body/eval_jaxpr/ppermute | solution.py:12
  168.0 16.7 %collective-permute-start.1 = (bf16[256,384]{0,1:T(8,128)(2,1)S(1)}, bf16[256,384]{0,1:T(8,128)(2,1)S(1)}, u32[]{:S(2)}, u32[]{:S(2)}) collective-permute-start(bf16[256,384]{0,1:T(8,128)(2,1)S(1)} %get-tuple-element.679), channel_id=1, source_target_pairs={{480,0},{0,32},{32,64},{64,96},{96,128},{128,160},{160,192},{192,2... | collective-permute-start | bytes 589832 | tf_op jit(solution)/shard_map/while/body/eval_jaxpr/ppermute | solution.py:12
  215.1 16.1 %collective-permute-start = (bf16[256,384]{0,1:T(8,128)(2,1)S(1)}, bf16[256,384]{0,1:T(8,128)(2,1)S(1)}, u32[]{:S(2)}, u32[]{:S(2)}) collective-permute-start(bf16[256,384]{0,1:T(8,128)(2,1)S(1)} %get-tuple-element.678), channel_id=1, source_target_pairs={{480,0},{0,32},{32,64},{64,96},{96,128},{128,160},{160,192},{192,2... | collective-permute-start | bytes 589832 | tf_op jit(solution)/shard_map/while/body/eval_jaxpr/ppermute | solution.py:12
  217.0 14.5 %collective-permute-start.1 = (bf16[256,384]{0,1:T(8,128)(2,1)S(1)}, bf16[256,384]{0,1:T(8,128)(2,1)S(1)}, u32[]{:S(2)}, u32[]{:S(2)}) collective-permute-start(bf16[256,384]{0,1:T(8,128)(2,1)S(1)} %get-tuple-element.679), channel_id=1, source_target_pairs={{480,0},{0,32},{32,64},{64,96},{96,128},{128,160},{160,192},{192,2... | collective-permute-start | bytes 589832 | tf_op jit(solution)/shard_map/while/body/eval_jaxpr/ppermute | solution.py:12
  256.8 23.8 %collective-permute-start = (bf16[256,384]{0,1:T(8,128)(2,1)S(1)}, bf16[256,384]{0,1:T(8,128)(2,1)S(1)}, u32[]{:S(2)}, u32[]{:S(2)}) collective-permute-start(bf16[256,384]{0,1:T(8,128)(2,1)S(1)} %get-tuple-element.678), channel_id=1, source_target_pairs={{480,0},{0,32},{32,64},{64,96},{96,128},{128,160},{160,192},{192,2... | collective-permute-start | bytes 589832 | tf_op jit(solution)/shard_map/while/body/eval_jaxpr/ppermute | solution.py:12
  262.2 18.7 %collective-permute-start.1 = (bf16[256,384]{0,1:T(8,128)(2,1)S(1)}, bf16[256,384]{0,1:T(8,128)(2,1)S(1)}, u32[]{:S(2)}, u32[]{:S(2)}) collective-permute-start(bf16[256,384]{0,1:T(8,128)(2,1)S(1)} %get-tuple-element.679), channel_id=1, source_target_pairs={{480,0},{0,32},{32,64},{64,96},{96,128},{128,160},{160,192},{192,2... | collective-permute-start | bytes 589832 | tf_op jit(solution)/shard_map/while/body/eval_jaxpr/ppermute | solution.py:12
  315.4 14.2 %collective-permute-start.4 = (f32[256,384]{0,1:T(8,128)S(1)}, f32[256,384]{0,1:T(8,128)S(1)}, u32[]{:S(2)}, u32[]{:S(2)}) collective-permute-start(f32[256,384]{0,1:T(8,128)S(1)} %get-tuple-element.682), channel_id=1, source_target_pairs={{480,0},{0,32},{32,64},{64,96},{96,128},{128,160},{160,192},{192,2... | collective-permute-start | bytes 1179656 | tf_op jit(solution)/shard_map/while/body/eval_jaxpr/ppermute | solution.py:12
  329.7 15.6 %collective-permute-start = (bf16[256,384]{0,1:T(8,128)(2,1)S(1)}, bf16[256,384]{0,1:T(8,128)(2,1)S(1)}, u32[]{:S(2)}, u32[]{:S(2)}) collective-permute-start(bf16[256,384]{0,1:T(8,128)(2,1)S(1)} %get-tuple-element.678), channel_id=1, source_target_pairs={{480,0},{0,32},{32,64},{64,96},{96,128},{128,160},{160,192},{192,2... | collective-permute-start | bytes 589832 | tf_op jit(solution)/shard_map/while/body/eval_jaxpr/ppermute | solution.py:12
  352.7 25.0 %collective-permute-start = (bf16[256,384]{0,1:T(8,128)(2,1)S(1)}, bf16[256,384]{0,1:T(8,128)(2,1)S(1)}, u32[]{:S(2)}, u32[]{:S(2)}) collective-permute-start(bf16[256,384]{0,1:T(8,128)(2,1)S(1)} %get-tuple-element.678), channel_id=1, source_target_pairs={{480,0},{0,32},{32,64},{64,96},{96,128},{128,160},{160,192},{192,2... | collective-permute-start | bytes 589832 | tf_op jit(solution)/shard_map/while/body/eval_jaxpr/ppermute | solution.py:12
  356.1 21.9 %collective-permute-start.1 = (bf16[256,384]{0,1:T(8,128)(2,1)S(1)}, bf16[256,384]{0,1:T(8,128)(2,1)S(1)}, u32[]{:S(2)}, u32[]{:S(2)}) collective-permute-start(bf16[256,384]{0,1:T(8,128)(2,1)S(1)} %get-tuple-element.679), channel_id=1, source_target_pairs={{480,0},{0,32},{32,64},{64,96},{96,128},{128,160},{160,192},{192,2... | collective-permute-start | bytes 589832 | tf_op jit(solution)/shard_map/while/body/eval_jaxpr/ppermute | solution.py:12
  363.3 14.3 %collective-permute-start.2 = (f32[3,256]{1,0:T(4,128)S(1)}, f32[3,256]{1,0:T(4,128)S(1)}, u32[]{:S(2)}, u32[]{:S(2)}) collective-permute-start(f32[3,256]{1,0:T(4,128)S(1)} %get-tuple-element.680), channel_id=1, source_target_pairs={{480,0},{0,32},{32,64},{64,96},{96,128},{128,160},{160,192},{192,2... | collective-permute-start | bytes 9224 | tf_op jit(solution)/shard_map/while/body/eval_jaxpr/ppermute | solution.py:12
  426.7 16.0 %collective-permute-start = (bf16[256,384]{0,1:T(8,128)(2,1)S(1)}, bf16[256,384]{0,1:T(8,128)(2,1)S(1)}, u32[]{:S(2)}, u32[]{:S(2)}) collective-permute-start(bf16[256,384]{0,1:T(8,128)(2,1)S(1)} %get-tuple-element.678), channel_id=1, source_target_pairs={{480,0},{0,32},{32,64},{64,96},{96,128},{128,160},{160,192},{192,2... | collective-permute-start | bytes 589832 | tf_op jit(solution)/shard_map/while/body/eval_jaxpr/ppermute | solution.py:12
  428.6 14.4 %collective-permute-start.1 = (bf16[256,384]{0,1:T(8,128)(2,1)S(1)}, bf16[256,384]{0,1:T(8,128)(2,1)S(1)}, u32[]{:S(2)}, u32[]{:S(2)}) collective-permute-start(bf16[256,384]{0,1:T(8,128)(2,1)S(1)} %get-tuple-element.679), channel_id=1, source_target_pairs={{480,0},{0,32},{32,64},{64,96},{96,128},{128,160},{160,192},{192,2... | collective-permute-start | bytes 589832 | tf_op jit(solution)/shard_map/while/body/eval_jaxpr/ppermute | solution.py:12
  447.2 30.4 %collective-permute-start = (bf16[256,384]{0,1:T(8,128)(2,1)S(1)}, bf16[256,384]{0,1:T(8,128)(2,1)S(1)}, u32[]{:S(2)}, u32[]{:S(2)}) collective-permute-start(bf16[256,384]{0,1:T(8,128)(2,1)S(1)} %get-tuple-element.678), channel_id=1, source_target_pairs={{480,0},{0,32},{32,64},{64,96},{96,128},{128,160},{160,192},{192,2... | collective-permute-start | bytes 589832 | tf_op jit(solution)/shard_map/while/body/eval_jaxpr/ppermute | solution.py:12
  453.8 24.2 %collective-permute-start.1 = (bf16[256,384]{0,1:T(8,128)(2,1)S(1)}, bf16[256,384]{0,1:T(8,128)(2,1)S(1)}, u32[]{:S(2)}, u32[]{:S(2)}) collective-permute-start(bf16[256,384]{0,1:T(8,128)(2,1)S(1)} %get-tuple-element.679), channel_id=1, source_target_pairs={{480,0},{0,32},{32,64},{64,96},{96,128},{128,160},{160,192},{192,2... | collective-permute-start | bytes 589832 | tf_op jit(solution)/shard_map/while/body/eval_jaxpr/ppermute | solution.py:12
  459.6 17.9 %collective-permute-start.2 = (f32[3,256]{1,0:T(4,128)S(1)}, f32[3,256]{1,0:T(4,128)S(1)}, u32[]{:S(2)}, u32[]{:S(2)}) collective-permute-start(f32[3,256]{1,0:T(4,128)S(1)} %get-tuple-element.680), channel_id=1, source_target_pairs={{480,0},{0,32},{32,64},{64,96},{96,128},{128,160},{160,192},{192,2... | collective-permute-start | bytes 9224 | tf_op jit(solution)/shard_map/while/body/eval_jaxpr/ppermute | solution.py:12
  507.4 31.5 %all-to-all-start.7 = ((bf16[8,2,2048]{2,1,0:T(2,128)(2,1)}), bf16[8,2,2048]{2,1,0:T(2,128)(2,1)S(1)}, u32[]{:S(2)}, u32[]{:S(2)}) async-start(bf16[8,2,2048]{2,1,0:T(2,128)(2,1)} %reshape.324), calls=%async_computation.7 | async-start | bytes 131072 | tf_op jit(solution)/shard_map/all_to_all | solution.py:153
  511.0 47.1 %collective-permute-start.6 = (bf16[1,32,3072]{2,1,0:T(8,128)(2,1)S(1)}, bf16[1,32,3072]{2,1,0:T(8,128)(2,1)S(1)}, u32[]{:S(2)}, u32[]{:S(2)}) collective-permute-start(bf16[1,32,3072]{2,1,0:T(8,128)(2,1)S(1)} %bitcast.295), channel_id=1, source_target_pairs={{1,0},{2,1},{3,2},{0,3},{5,4},{6,5},{7,6},{4,7},{9,8},{10,9},{11,1... | collective-permute-start | bytes 589832 | tf_op jit(solution)/shard_map/ppermute | solution.py:12
  (68 other events, 758.1 us)
where the time goes:
time: 564 us; the launch traced here: 560 us
  starting transfers between devices  302 us (54%)
  waiting for transfers between devices  129 us (23%)
  other arithmetic  47.9 us (8%)
  local copies, waits for them, and re-layouts  32.8 us (6%)
  loops' own time  22.3 us (4%)
  matrix products  21.7 us (4%)
    ppermute x79, starting transfers between devices, shifted(): return lax.ppermute(block, axis, route)  258 us
    ppermute x79, waiting for transfers between devices, shifted(): return lax.ppermute(block, axis, route)  98.7 us
    unnamed x7, other arithmetic  42.5 us
    another operation x1, loops' own time, body(): lax.fori_loop(1, ctx_size, query_turn, (query_local, grad_local, lse_loca...  22.3 us
    unnamed x40, local copies, waits for them, and re-layouts  17.6 us
  transfers between devices with their start and end apart: 88, of which 28 were waited for; matrix products, arithmetic and copies ran while one was open for 17% of the time, Pallas kernels for 0%

commit v1 on v0

v1 whole, which is shorter than its diff:
```python
import functools

import jax
import jax.numpy as jnp
from jax import lax
from jax.experimental import pallas as pl
from jax.experimental.pallas import tpu as pltpu
from jax.sharding import PartitionSpec as P

D = 128
BLOCK = 128
GROUP = 3
LOG2E = 1.4426950408889634
MESH = pl.DeviceIdType.MESH


def kernel(
    sizes,
    lens,
    table,
    q_in,
    k_in,
    v_in,
    g_in,
    lse_in,
    delta_in,
    gq_out,
    gk_out,
    gv_out,
    q_own,
    g_own,
    q_stack,
    g_stack,
    q_turned,
    g_turned,
    kv,
    lse_raw,
    delta_raw,
    stat_out,
    stat_in,
    stat,
    dq,
    part,
    chain,
    oq,
    ok,
    ov,
    raw_sem,
    kv_sem,
    q_sem,
    g_sem,
    stat_sem,
    in_send,
    ag_send,
    ag_recv,
    rs_send,
    rs_recv,
    out_send,
    out_recv,
):
    n, heads, sections = sizes
    half = n // 2
    rows = q_in.shape[1]
    per_block = BLOCK // rows
    width = GROUP * D
    scale = D ** (-0.5)
    me = lax.axis_index("ctx")
    head = lax.axis_index("head")
    section = lax.axis_index("section")
    right, left = lax.rem(me + 1, n), lax.rem(me + n - 1, n)
    neighbour = (right, left)

    raw_lse = pltpu.make_async_copy(lse_in.at[0], lse_raw, raw_sem.at[0])
    raw_delta = pltpu.make_async_copy(delta_in.at[0], delta_raw, raw_sem.at[1])
    raw_lse.start()
    raw_delta.start()

    barrier = pltpu.get_barrier_semaphore()

    def greet(o, carry):
        pl.semaphore_signal(
            barrier, inc=1, device_id={"head": lax.rem(head + o, heads)}, device_id_type=MESH
        )
        return carry

    def greet_next(o, carry):
        pl.semaphore_signal(
            barrier,
            inc=1,
            device_id={
                "head": lax.rem(head + o, heads),
                "section": lax.rem(section + 1, sections),
            },
            device_id_type=MESH,
        )
        return carry

    lax.fori_loop(1, heads, greet, 0)
    for other in neighbour:
        pl.semaphore_signal(barrier, inc=1, device_id={"ctx": other}, device_id_type=MESH)
    lax.fori_loop(0, heads, greet_next, 0)
    pl.semaphore_wait(barrier, 2 * heads + 1)

    block_of, row_of = head // per_block, (head % per_block) * rows
    stat_half = rows * (head % per_block)

    def to_peer(src, dst, slot, sem, peer):
        return pltpu.make_async_remote_copy(
            src_ref=src,
            dst_ref=dst,
            send_sem=slot,
            recv_sem=sem,
            device_id={"head": peer},
            device_id_type=MESH,
        )

    def kv_slot(which):
        return kv.at[me, block_of, which, pl.ds(pl.multiple_of(row_of, rows), rows)]

    def kv_copies(o, peer):
        columns = pl.ds(pl.multiple_of(peer * D, D), D)
        return (
            to_peer(k_in.at[0, :, columns], kv_slot(0), in_send.at[0, o], kv_sem, peer),
            to_peer(v_in.at[0, :, columns], kv_slot(1), in_send.at[1, o], kv_sem, peer),
        )

    def wide_copies(o, peer):
        columns = pl.ds(pl.multiple_of(peer * width, width), width)
        own_rows = pl.ds(pl.multiple_of(head * rows, rows), rows)
        return (
            to_peer(q_in.at[0, :, columns], q_own.at[own_rows], in_send.at[2, o], q_sem, peer),
            to_peer(g_in.at[0, :, columns], g_own.at[own_rows], in_send.at[3, o], g_sem, peer),
        )

    def stat_copy(o, peer):
        return to_peer(stat_out.at[peer], stat_in.at[head], in_send.at[4, o], stat_sem, peer)

    def start_kv(o, carry):
        for copy in kv_copies(o, lax.rem(head + o, heads)):
            copy.start()
        return carry

    def start_wide(o, carry):
        for copy in wide_copies(o, lax.rem(head + o, heads)):
            copy.start()
        return carry

    def start_stat(o, carry):
        stat_copy(o, lax.rem(head + o, heads)).start()
        return carry

    def end_in(o, carry):
        peer = lax.rem(head + o, heads)
        for copy in kv_copies(o, peer) + wide_copies(o, peer) + (stat_copy(o, peer),):
            copy.wait_send()
        return carry

    lax.fori_loop(1, heads, start_kv, 0)
    own_narrow = pl.ds(pl.multiple_of(head * D, D), D)
    own_wide = pl.ds(pl.multiple_of(head * width, width), width)
    own_rows = pl.ds(pl.multiple_of(head * rows, rows), rows)
    pltpu.make_async_copy(k_in.at[0, :, own_narrow], kv_slot(0), kv_sem).start()
    pltpu.make_async_copy(v_in.at[0, :, own_narrow], kv_slot(1), kv_sem).start()
    lax.fori_loop(1, heads, start_wide, 0)
    pltpu.make_async_copy(q_in.at[0, :, own_wide], q_own.at[own_rows], q_sem).start()
    pltpu.make_async_copy(g_in.at[0, :, own_wide], g_own.at[own_rows], g_sem).start()

    raw_lse.wait()
    raw_delta.wait()
    lanes = lax.broadcasted_iota(jnp.int32, (1, BLOCK), 1)
    mine = (lanes >= stat_half) & (lanes < stat_half + rows)
    spread_lse = jnp.where(mine, jnp.concatenate([lse_raw[...]] * per_block, axis=1), 0.0)
    spread_delta = jnp.where(mine, jnp.concatenate([delta_raw[...]] * per_block, axis=1), 0.0)
    stat_out[...] = jnp.zeros_like(stat_out)
    for p in range(heads):
        stat_out[p, 0:GROUP] = spread_lse[p * GROUP : (p + 1) * GROUP] * LOG2E
        stat_out[p, GROUP : 2 * GROUP] = spread_delta[p * GROUP : (p + 1) * GROUP]
    lax.fori_loop(1, heads, start_stat, 0)
    pltpu.make_async_copy(stat_out.at[head], stat_in.at[head], stat_sem).start()

    def source(hops, d):
        return lax.rem(me + (n - hops if d == 0 else hops), n)

    def ag_copy(hop, d, c):
        slot = source(hop - 1, d)
        return pltpu.make_async_remote_copy(
            src_ref=kv.at[slot, c],
            dst_ref=kv.at[slot, c],
            send_sem=ag_send.at[d, c, hop],
            recv_sem=ag_recv.at[d, c, hop],
            device_id={"ctx": neighbour[d]},
            device_id_type=MESH,
        )

    def ag_arrived(hop, d, c):
        slot = source(hop, d)
        pltpu.make_async_copy(kv.at[slot, c], kv.at[slot, c], ag_recv.at[d, c, hop]).wait()

    pltpu.make_async_copy(kv.at[me], kv.at[me], kv_sem).wait()
    for c in range(2):
        for d in range(2):
            ag_copy(1, d, c).start()

    def lay_out():
        pltpu.make_async_copy(q_own, q_own, q_sem).wait()
        pltpu.make_async_copy(g_own, g_own, g_sem).wait()
        pltpu.make_async_copy(stat_in, stat_in, stat_sem).wait()
        for b in range(2):
            for h in range(GROUP):
                piece = slice((b * GROUP + h) * BLOCK, (b * GROUP + h + 1) * BLOCK)
                for own, stack, turned in (
                    (q_own, q_stack, q_turned),
                    (g_own, g_stack, g_turned),
                ):
                    tile = own[b * BLOCK : (b + 1) * BLOCK, h * D : (h + 1) * D]
                    stack[piece, :] = tile
                    turned[:, piece] = tile.T
            first = b * per_block
            total = stat_in[first]
            for p in range(1, per_block):
                total = total + stat_in[first + p]
            stat[b] = total
        dq[...] = jnp.zeros_like(dq)

    ends = [lens[0, 0]]
    for i in range(1, lens.shape[1]):
        ends.append(ends[-1] + lens[0, i])
    query_places, query_starts = [], []
    for b in range(2):
        places = table[me, b] * BLOCK + lanes
        starts = jnp.zeros_like(places)
        for end in ends:
            starts = jnp.where(places >= end, jnp.maximum(starts, end), starts)
        query_places.append(places)
        query_starts.append(starts)
    key_offsets = lax.broadcasted_iota(jnp.int32, (BLOCK, BLOCK), 0)

    def visit(j):
        for c in range(2):
            keys, values = kv[j, c, 0], kv[j, c, 1]
            pieces = slice(c * width, 2 * width)
            scores = jnp.dot(keys, q_turned[:, pieces], preferred_element_type=jnp.float32)
            grads = jnp.dot(values, g_turned[:, pieces], preferred_element_type=jnp.float32)
            key_places = table[j, c] * BLOCK + key_offsets
            weights, dscores = [], []
            for b in range(c, 2):
                live = (key_places <= query_places[b]) & (key_places >= query_starts[b])
                for h in range(GROUP):
                    at = ((b - c) * GROUP + h) * BLOCK
                    x = scores[:, at : at + BLOCK] * (scale * LOG2E) - stat[b, h : h + 1, :]
                    weight = jnp.where(live, jnp.exp2(x), 0.0)
                    dscore = weight * (
                        grads[:, at : at + BLOCK] - stat[b, GROUP + h : GROUP + h + 1, :]
                    )
                    weights.append(weight.astype(jnp.bfloat16))
                    dscores.append(dscore.astype(jnp.bfloat16))
            weight16 = jnp.concatenate(weights, axis=1)
            dscore16 = jnp.concatenate(dscores, axis=1)
            part[j, c, 0] = jnp.dot(
                dscore16, q_stack[pieces, :], preferred_element_type=jnp.float32
            )
            part[j, c, 1] = jnp.dot(
                weight16, g_stack[pieces, :], preferred_element_type=jnp.float32
            )
            dq[:, pieces] += jnp.dot(keys.T, dscore16, preferred_element_type=jnp.float32)

    def visit_number(i, carry):
        distance = (i + 1) // 2
        visit(lax.rem(me + n + distance * (2 * (i % 2) - 1), n))
        return carry

    per_turn = 3
    first_turn = half - (n - 1) // per_turn

    def forward(hop, last):
        for c in range(2):
            for d in range(2):
                ag_arrived(hop, d, c)
                if not last or c == d:
                    ag_copy(hop + 1, d, c).start()

    def turn(hop, carry):
        forward(hop, False)
        first = (hop - first_turn) * per_turn
        lax.fori_loop(first, first + per_turn, visit_number, 0)
        return carry

    def idle_turn(hop, carry):
        forward(hop, False)
        return carry

    lax.fori_loop(1, first_turn, idle_turn, 0)
    lay_out()
    lax.fori_loop(first_turn, half - 1, turn, 0)
    forward(half - 1, True)
    lax.fori_loop(n - 1 - per_turn, n - 1, visit_number, 0)

    def hops_of(d, c):
        return half if c == d else half - 1

    def rs_target(t, d, c):
        return source(n - (hops_of(d, c) + 1 - t), d)

    def rs_copy(t, d, c):
        return pltpu.make_async_remote_copy(
            src_ref=chain.at[d, c, t - 1],
            dst_ref=chain.at[d, c, t],
            send_sem=rs_send.at[d, c, t],
            recv_sem=rs_recv.at[d, c, t],
            device_id={"ctx": neighbour[d]},
            device_id_type=MESH,
        )

    def rs_arrived(t, d, c):
        pltpu.make_async_copy(chain.at[d, c, t], chain.at[d, c, t], rs_recv.at[d, c, t]).wait()

    def rs_begin(d, c):
        chain[d, c, 0] = part[rs_target(1, d, c), c].astype(jnp.bfloat16)
        rs_copy(1, d, c).start()

    def rs_pass(t, d, c):
        rs_arrived(t - 1, d, c)
        total = chain[d, c, t - 1].astype(jnp.float32) + part[rs_target(t, d, c), c]
        chain[d, c, t - 1] = total.astype(jnp.bfloat16)
        rs_copy(t, d, c).start()

    rs_begin(0, 1)
    rs_begin(1, 0)
    for c in range(2):
        ag_arrived(half, c, c)
    visit(lax.rem(me + half, n))
    rs_begin(0, 0)
    rs_begin(1, 1)

    down = lax.rem(section + sections - 1, sections)

    def out_copy(array, src, dst, columns, o):
        peer = lax.rem(head + o, heads)
        return pltpu.make_async_remote_copy(
            src_ref=src.at[pl.ds(pl.multiple_of(peer * rows, rows), rows)],
            dst_ref=dst.at[0, :, columns],
            send_sem=out_send.at[array, o],
            recv_sem=out_recv.at[array],
            device_id={"head": peer, "section": down},
            device_id_type=MESH,
        )

    for b in range(2):
        for h in range(GROUP):
            piece = slice((b * GROUP + h) * BLOCK, (b * GROUP + h + 1) * BLOCK)
            oq[b * BLOCK : (b + 1) * BLOCK, h * D : (h + 1) * D] = (
                (dq[:, piece] * scale).T.astype(jnp.bfloat16)
            )

    def start_query(o, carry):
        out_copy(0, oq, gq_out, own_wide, o).start()
        return carry

    lax.fori_loop(0, heads, start_query, 0)

    def rs_turn(t, carry):
        for d in range(2):
            rs_pass(t, d, 1 - d)
        for d in range(2):
            rs_pass(t, d, d)
        return carry

    lax.fori_loop(2, half, rs_turn, 0)
    for d in range(2):
        rs_pass(half, d, d)
    for d in range(2):
        rs_arrived(half - 1, d, 1 - d)
    for d in range(2):
        rs_arrived(half, d, d)
    for c in range(2):
        total = part[me, c]
        for d in range(2):
            total = total + chain[d, c, hops_of(d, c)].astype(jnp.float32)
        ok[c * BLOCK : (c + 1) * BLOCK, :] = (total[0] * scale).astype(jnp.bfloat16)
        ov[c * BLOCK : (c + 1) * BLOCK, :] = total[1].astype(jnp.bfloat16)

    def start_narrow(o, carry):
        out_copy(1, ok, gk_out, own_narrow, o).start()
        out_copy(2, ov, gv_out, own_narrow, o).start()
        return carry

    lax.fori_loop(0, heads, start_narrow, 0)

    lax.fori_loop(1, heads, end_in, 0)

    def end_ring(t, carry):
        for c in range(2):
            for d in range(2):
                ag_copy(t, d, c).wait_send()
                rs_copy(t, d, c).wait_send()
        return carry

    lax.fori_loop(1, half, end_ring, 0)
    for d in range(2):
        ag_copy(half, d, d).wait_send()
        rs_copy(half, d, d).wait_send()

    def end_out(o, carry):
        out_copy(0, oq, gq_out, own_wide, o).wait_send()
        out_copy(1, ok, gk_out, own_narrow, o).wait_send()
        out_copy(2, ov, gv_out, own_narrow, o).wait_send()
        return carry

    lax.fori_loop(0, heads, end_out, 0)
    for array, out in enumerate((gq_out, gk_out, gv_out)):
        pltpu.make_async_copy(out, out, out_recv.at[array]).wait()


def body(sizes, q, k, v, g, lse, delta, lens, table):
    n, heads, _ = sizes
    half = n // 2
    rows = q.shape[1]
    tokens = rows * heads
    bf16, f32 = jnp.bfloat16, jnp.float32
    any_space = pl.BlockSpec(memory_space=pl.ANY)
    smem = pl.BlockSpec(memory_space=pltpu.SMEM)
    dma = pltpu.SemaphoreType.DMA
    pieces = tokens * GROUP
    return pl.pallas_call(
        functools.partial(kernel, sizes),
        out_shape=(
            jax.ShapeDtypeStruct(q.shape, bf16),
            jax.ShapeDtypeStruct(k.shape, bf16),
            jax.ShapeDtypeStruct(v.shape, bf16),
        ),
        in_specs=[smem, smem] + [any_space] * 6,
        out_specs=(any_space,) * 3,
        scratch_shapes=[
            pltpu.VMEM((tokens, GROUP * D), bf16),
            pltpu.VMEM((tokens, GROUP * D), bf16),
            pltpu.VMEM((pieces, D), bf16),
            pltpu.VMEM((pieces, D), bf16),
            pltpu.VMEM((D, pieces), bf16),
            pltpu.VMEM((D, pieces), bf16),
            pltpu.VMEM((n, 2, 2, BLOCK, D), bf16),
            pltpu.VMEM((lse.shape[1], rows), f32),
            pltpu.VMEM((lse.shape[1], rows), f32),
            pltpu.VMEM((heads, 8, BLOCK), f32),
            pltpu.VMEM((heads, 8, BLOCK), f32),
            pltpu.VMEM((2, 8, BLOCK), f32),
            pltpu.VMEM((D, pieces), f32),
            pltpu.VMEM((n, 2, 2, BLOCK, D), f32),
            pltpu.VMEM((2, 2, half + 1, 2, BLOCK, D), bf16),
            pltpu.VMEM((tokens, GROUP * D), bf16),
            pltpu.VMEM((tokens, D), bf16),
            pltpu.VMEM((tokens, D), bf16),
            dma((2,)),
            dma,
            dma,
            dma,
            dma,
            dma((5, heads)),
            dma((2, 2, half + 1)),
            dma((2, 2, half + 1)),
            dma((2, 2, half + 1)),
            dma((2, 2, half + 1)),
            dma((3, heads)),
            dma((3,)),
        ],
        compiler_params=pltpu.CompilerParams(
            collective_id=0, has_side_effects=True, vmem_limit_bytes=40 * 1024 * 1024
        ),
    )(lens, table, q, k, v, g, lse, delta)


def solution(mesh):
    sizes = (mesh.shape["ctx"], mesh.shape["head"], mesh.shape["section"])
    tokens = P("section", ("ctx", "head"), None)
    totals = P("section", None, ("ctx", "head"))
    return jax.shard_map(
        functools.partial(body, sizes),
        mesh=mesh,
        in_specs=(tokens, tokens, tokens, tokens, totals, totals, P("section", None), P()),
        out_specs=(tokens, tokens, tokens),
        check_vma=False,
    )
```

time: 564 us -> 99.8 us (0.18)
  starting transfers between devices: 302 us -> 0 us
  waiting for transfers between devices: 129 us -> 0 us
  Pallas kernels: 0 us -> 91.1 us
  other arithmetic: 47.9 us -> 0 us
  local copies, waits for them, and re-layouts: 32.8 us -> 7.65 us
  loops' own time: 22.3 us -> 0 us
  matrix products: 21.7 us -> 0 us
    ppermute x79 -> x0, starting transfers between devices: 258 us -> none  [shifted(): return lax.ppermute(block, axis, route)]
    ppermute x79 -> x0, waiting for transfers between devices: 98.7 us -> none  [shifted(): return lax.ppermute(block, axis, route)]
    pallas_call x0 -> x1, Pallas kernels: none -> 91.1 us  [body(): pl.pallas_call(functools.partial(kernel, sizes), out_shape=(jax.ShapeDtyp...]
    all_to_all x9 -> x0, starting transfers between devices: 44.6 us -> none  [the longest x1 7.62 us: body(): lax.all_to_all(log_sum_exp, 'head', split_axis=1, concat_axis=2, tiled=True)]
    unnamed x7 -> x0, other arithmetic: 42.5 us -> none
    all_to_all x9 -> x0, waiting for transfers between devices: 30.5 us -> none  [the longest x1 6.41 us: body(): lax.all_to_all(query_rows, 'head', split_axis=2, concat_axis=1, tiled=True)]
    another operation x1 -> x0, loops' own time: 22.3 us -> none  [body(): lax.fori_loop(1, ctx_size, query_turn, (query_local, grad_local, lse_loca...]
    dot_general x80 -> x0, matrix products: 21.7 us -> none  [the longest x16 5.46 us: block_terms(): jnp.einsum('ikgd,jkd->kgij', query_heads, key_heads, preferred_element_ty...]
  transfers between devices with their start and end apart: 88 -> 0, of which waited for: 28 -> 0; matrix products, arithmetic and copies ran while one was open for 17% -> 0% of each run, Pallas kernels for 0% -> 0%
where the time goes in v1:
time: 99.8 us; the launch traced here: 99.4 us
  Pallas kernels  91.1 us (91%)
  local copies, waits for them, and re-layouts  7.65 us (8%)
    pallas_call x1, Pallas kernels, body(): pl.pallas_call(functools.partial(kernel, sizes), out_shape=(jax.ShapeDtyp...  91.1 us
    unnamed x18, local copies, waits for them, and re-layouts  7.65 us

profile of v1, /device:TPU:1, one launch (start us, length us, event | category | flops | bytes accessed | tf_op | source)
XLA Modules:
  0.0 99.4 jit_solution(3490883238969839191)
XLA Ops:
  0.6 0.0 copy-start.6
  0.6 0.8 copy.11.table
  1.4 0.0 copy-done.6
  1.4 0.0 copy-start
  1.4 0.9 copy-done
  2.3 0.0 copy-start.1
  2.3 0.9 copy-done.1
  3.3 0.0 copy-start.2
  3.3 0.8 copy-done.2
  4.1 0.0 copy-start.3
  4.1 0.8 copy-done.3
  4.9 0.0 copy-start.4
  4.9 0.7 copy-done.4
  5.6 0.0 copy-start.5
  5.6 0.7 copy-done.5
  6.4 91.1 %shard_map.103 = (bf16[1,32,3072]{2,1,0:T(8,128)(2,1)S(1)}, bf16[1,32,1024]{2,1,0:T(8,128)(2,1)S(1)}, bf16[1,32,1024]{2,1,0:T(8,128)(2,1)S(1)}) custom-call(s32[1,4]{1,0:T(1,128)S(1)} %copy-done.6, s32[16,2]{1,0:T(8,128)S(1)} %copy.11.table, bf16[1,32,3072]{2,1,0:T(8,128)(2,1)S(1)} %copy-done, bf16[1,32,1024]{2,1,0:T(8,128)(2,1)S(1)} %copy-done.2, ...), custom_call_target="tpu_custom_call" | custom-call | tf_op jit(solution)/shard_map/pallas_call | solution.py:424
  97.5 0.7 copy.15
  98.2 0.6 copy.16
  98.8 0.6 copy.17
Async XLA Ops:
  0.6 0.8 copy-start.6
  1.4 0.9 copy-start
  2.3 0.9 copy-start.1
  3.3 0.8 copy-start.2
  4.1 0.8 copy-start.3
  4.9 0.7 copy-start.4
  5.6 0.7 copy-start.5

commit v2 on v0

v2 whole, which is shorter than its diff:
```python
import functools

import jax
import jax.numpy as jnp
from jax import lax
from jax.experimental import pallas as pl
from jax.experimental.pallas import tpu as pltpu
from jax.sharding import PartitionSpec as P

D = 128
BLOCK = 128
GROUP = 3
RING = 4
PEERS = 8
RUN = 64
LOG2E = 1.4426950408889634
MESH = pl.DeviceIdType.MESH


def order_of(i):
    along_y = (0, 0, 0, 1, 1, 1, 3, 3, 3, 0, 1, 3, 2, 2, 2, 2)
    along_z = (0, 1, 3, 0, 1, 3, 0, 1, 3, 2, 2, 2, 2, 1, 3, 0)
    dy = sum(jnp.where(i == k, v, 0) for k, v in enumerate(along_y) if v)
    dr = sum(jnp.where(i == k, v, 0) for k, v in enumerate(along_z) if v)
    return dy, dr


def kernel(
    lens,
    table,
    q_in,
    k_in,
    v_in,
    g_in,
    lse_in,
    delta_in,
    gq_out,
    gk_out,
    gv_out,
    qg,
    q_stack,
    g_stack,
    q_turned,
    g_turned,
    kv,
    lse_raw,
    delta_raw,
    stat_out,
    stat_in,
    stat,
    dq,
    part,
    zs1,
    zr1,
    zs2,
    zr2,
    ys1,
    yr1,
    ys2,
    yr2,
    oq,
    okv,
    raw_sem,
    kv_sem,
    q_sem,
    stat_sem,
    in_send,
    ag1_send,
    ag1_recv,
    ag2_send,
    ag2_recv,
    yq1_send,
    yq1_recv,
    yq2_send,
    yq2_recv,
    yt_send,
    yt_recv,
    z1_send,
    z1_recv,
    z2_send,
    z2_recv,
    y1_send,
    y1_recv,
    y2_send,
    y2_recv,
    out_send,
    out_recv,
):
    rows = q_in.shape[1]
    width = GROUP * D
    scale = D ** (-0.5)
    sections = lax.axis_size("section")
    z, place, section = lax.axis_index("ctx"), lax.axis_index("head"), lax.axis_index("section")
    region, plane = z // RING, z % RING
    y, x = place // 2, place % 2
    mine = plane * 2 + x

    def peer_id(p):
        return {"ctx": region * RING + p // 2, "head": y * 2 + p % 2}

    def z_id(d):
        return {"ctx": lax.rem(z + (RING if d == 0 else 3 * RING), RING * RING)}

    def y_id(o):
        return {"head": lax.rem(y + o, RING) * 2 + x}

    y_step = (1, 3)

    def remote(src, dst, send, recv, where):
        return pltpu.make_async_remote_copy(
            src_ref=src,
            dst_ref=dst,
            send_sem=send,
            recv_sem=recv,
            device_id=where,
            device_id_type=MESH,
        )

    def landed(ref, sem):
        pltpu.make_async_copy(ref, ref, sem).wait()

    raw_lse = pltpu.make_async_copy(lse_in.at[0], lse_raw, raw_sem.at[0])
    raw_delta = pltpu.make_async_copy(delta_in.at[0], delta_raw, raw_sem.at[1])
    raw_lse.start()
    raw_delta.start()

    barrier = pltpu.get_barrier_semaphore()

    def greet(where):
        pl.semaphore_signal(barrier, inc=1, device_id=where, device_id_type=MESH)

    def greet_peer(o, carry):
        greet(peer_id(lax.rem(mine + o, PEERS)))
        return carry

    def greet_up(o, carry):
        greet({**peer_id(lax.rem(mine + o, PEERS)), "section": lax.rem(section + 1, sections)})
        return carry

    lax.fori_loop(1, PEERS, greet_peer, 0)
    for d in range(2):
        greet(z_id(d))
    for o in range(1, RING):
        greet(y_id(o))
    lax.fori_loop(0, PEERS, greet_up, 0)

    part[...] = jnp.zeros_like(part)
    dq[...] = jnp.zeros_like(dq)
    stat_out[...] = jnp.zeros_like(stat_out)
    raw_lse.wait()
    raw_delta.wait()
    lanes = lax.broadcasted_iota(jnp.int32, (1, BLOCK), 1)
    per_tile = BLOCK // rows
    first_lane = rows * (mine % per_tile)
    own_lanes = (lanes >= first_lane) & (lanes < first_lane + rows)
    spread_lse = jnp.where(own_lanes, jnp.concatenate([lse_raw[...]] * per_tile, axis=1), 0.0)
    spread_delta = jnp.where(own_lanes, jnp.concatenate([delta_raw[...]] * per_tile, axis=1), 0.0)
    for p in range(PEERS):
        stat_out[p, 0:GROUP] = spread_lse[p * GROUP : (p + 1) * GROUP] * LOG2E
        stat_out[p, GROUP : 2 * GROUP] = spread_delta[p * GROUP : (p + 1) * GROUP]
    pl.semaphore_wait(barrier, 2 * PEERS - 1 + 2 + RING - 1)

    own_rows = pl.ds(pl.multiple_of(mine * rows, rows), rows)

    def narrow(p):
        return pl.ds(pl.multiple_of(p * D, D), D)

    def wide(p):
        return pl.ds(pl.multiple_of(p * width, width), width)

    def kv_copies(p):
        return tuple(
            remote(src.at[0, :, narrow(p)], kv.at[region, i, own_rows], in_send.at[i, p], kv_sem, peer_id(p))
            for i, src in enumerate((k_in, v_in))
        )

    def q_copies(p):
        return tuple(
            remote(src.at[0, :, wide(p)], qg.at[y, mine, i], in_send.at[2 + i, p], q_sem.at[mine], peer_id(p))
            for i, src in enumerate((q_in, g_in))
        )

    def stat_copies(p):
        return (remote(stat_out.at[p], stat_in.at[mine], in_send.at[4, p], stat_sem, peer_id(p)),)

    def to_peers(copies):
        def one(o, carry):
            for copy in copies(lax.rem(mine + o, PEERS)):
                copy.start()
            return carry

        lax.fori_loop(1, PEERS, one, 0)

    to_peers(kv_copies)
    for i, src in enumerate((k_in, v_in)):
        pltpu.make_async_copy(src.at[0, :, narrow(mine)], kv.at[region, i, own_rows], kv_sem).start()
    to_peers(stat_copies)
    pltpu.make_async_copy(stat_out.at[mine], stat_in.at[mine], stat_sem).start()
    to_peers(q_copies)
    for i, src in enumerate((q_in, g_in)):
        pltpu.make_async_copy(src.at[0, :, wide(mine)], qg.at[y, mine, i], q_sem.at[mine]).start()

    def region_at(o):
        return lax.rem(region + o, RING)

    def ag1(d, i):
        return remote(
            kv.at[region, i], kv.at[region, i], ag1_send.at[d, i], ag1_recv.at[d, i], z_id(d)
        )

    def ag1_landed(d, i):
        landed(kv.at[region_at(3 if d == 0 else 1), i], ag1_recv.at[d, i])

    def ag2(d):
        held = kv.at[region_at(3 if d == 0 else 1), d]
        return remote(held, held, ag2_send.at[d], ag2_recv.at[d], z_id(d))

    landed(kv.at[region], kv_sem)
    for i in range(2):
        for d in range(2):
            ag1(d, (i + d) % 2).start()

    def y_at(o):
        return lax.rem(y + o, RING)

    def yq1(p, d):
        held = qg.at[y, p]
        return remote(held, held, yq1_send.at[d, p], yq1_recv.at[d, p], y_id(y_step[d]))

    def yq1_landed(p, d):
        landed(qg.at[y_at(3 if d == 0 else 1), p], yq1_recv.at[d, p])

    def yq2(p, d):
        held = qg.at[y_at(3 if d == 0 else 1), p]
        return remote(held, held, yq2_send.at[p], yq2_recv.at[p], y_id(y_step[d]))

    def yt(o):
        return remote(stat.at[y], stat.at[y], yt_send.at[o], yt_recv.at[o], y_id(o))

    landed(stat_in, stat_sem)
    for b in range(2):
        first = b * per_tile
        total = stat_in[first]
        for p in range(1, per_tile):
            total = total + stat_in[first + p]
        stat[y, b] = total
    for o in range(1, RING):
        yt(o).start()

    def pass_own(p, carry):
        landed(qg.at[y, p], q_sem.at[p])
        for d in range(2):
            yq1(p, d).start()
        return carry

    lax.fori_loop(0, PEERS, pass_own, 0)

    def lay_out(at):
        for b in range(2):
            for i, stack, turned in ((0, q_stack, q_turned), (1, g_stack, g_turned)):
                tile = qg[at, b * per_tile : (b + 1) * per_tile, i].reshape(BLOCK, width)
                for h in range(GROUP):
                    piece = slice((b * GROUP + h) * BLOCK, (b * GROUP + h + 1) * BLOCK)
                    own = tile[:, h * D : (h + 1) * D]
                    stack[at, piece, :] = own
                    turned[at, :, piece] = own.T

    ends = [lens[0, 0]]
    for i in range(1, lens.shape[1]):
        ends.append(ends[-1] + lens[0, i])
    run_lanes = lanes % RUN
    run_rows = lax.broadcasted_iota(jnp.int32, (RUN, BLOCK), 0)

    def visit(yq, r):
        key_start = (y % 2) * RUN
        key_places = jnp.concatenate(
            [table[r * RING + u, y // 2] * BLOCK + key_start + run_rows for u in range(RING)], axis=0
        )
        keys, values = kv[r, 0], kv[r, 1]
        turned_keys = keys.T
        for b in range(2):
            half = slice(b * width, (b + 1) * width)
            starts_at = [table[region * RING + 2 * b + u, yq // 2] * BLOCK for u in range(2)]
            places = jnp.where(lanes < RUN, starts_at[0], starts_at[1]) + (yq % 2) * RUN + run_lanes
            starts = jnp.zeros_like(places)
            for end in ends:
                starts = jnp.where(places >= end, jnp.maximum(starts, end), starts)
            live = (key_places <= places) & (key_places >= starts)
            scores = jnp.dot(keys, q_turned[yq, :, half], preferred_element_type=jnp.float32)
            grads = jnp.dot(values, g_turned[yq, :, half], preferred_element_type=jnp.float32)
            totals = stat[yq, b]
            weights, dscores = [], []
            for h in range(GROUP):
                at = slice(h * BLOCK, (h + 1) * BLOCK)
                exponent = scores[:, at] * (scale * LOG2E) - totals[h : h + 1, :]
                weight = jnp.where(live, jnp.exp2(exponent), 0.0)
                dscore = weight * (grads[:, at] - totals[GROUP + h : GROUP + h + 1, :])
                weights.append(weight.astype(jnp.bfloat16))
                dscores.append(dscore.astype(jnp.bfloat16))
            weight16 = jnp.concatenate(weights, axis=1)
            dscore16 = jnp.concatenate(dscores, axis=1)
            part[r, 0] += jnp.dot(dscore16, q_stack[yq, half, :], preferred_element_type=jnp.float32)
            part[r, 1] += jnp.dot(weight16, g_stack[yq, half, :], preferred_element_type=jnp.float32)
            dq[yq, b] += jnp.dot(turned_keys, dscore16, preferred_element_type=jnp.float32)

    def z1(d):
        return remote(zs1.at[d], zr1.at[d], z1_send.at[d], z1_recv.at[d], z_id(d))

    def z2(d, i):
        return remote(zs2.at[d, i], zr2.at[d, i], z2_send.at[d, i], z2_recv.at[d, i], z_id(d))

    def y1(d):
        return remote(ys1.at[d], yr1.at[d], y1_send.at[d], y1_recv.at[d], y_id(y_step[d]))

    def y2(d, b):
        return remote(ys2.at[d, b], yr2.at[d, b], y2_send.at[d, b], y2_recv.at[d, b], y_id(y_step[d]))

    def turn(i, carry):
        dy, dr = order_of(i)

        @pl.when(i == 1)
        def _():
            for d in range(2):
                ag1_landed(d, d)
                ag2(d).start()
            for p in range(PEERS):
                yq1_landed(p, p % 2)
                yq2(p, p % 2).start()
            for d in range(2):
                ag1_landed(d, 1 - d)

        @pl.when(i == 3)
        def _():
            for p in range(0, PEERS, 2):
                yq1_landed(p, 1)
            landed(stat.at[y_at(1)], yt_recv.at[3])

        @pl.when(i == 6)
        def _():
            for p in range(1, PEERS, 2):
                yq1_landed(p, 0)
            landed(stat.at[y_at(3)], yt_recv.at[1])

        @pl.when(i == 9)
        def _():
            for d in range(2):
                landed(kv.at[region_at(2), d], ag2_recv.at[d])

        @pl.when(i == 12)
        def _():
            for p in range(PEERS):
                landed(qg.at[y_at(2), p], yq2_recv.at[p])
            landed(stat.at[y_at(2)], yt_recv.at[2])

        yq, r = y_at(dy), region_at(dr)

        @pl.when((i == 0) | (i == 3) | (i == 6) | (i == 12))
        def _():
            lay_out(yq)

        @pl.when((y < 2) | (yq >= 2))
        def _():
            visit(yq, r)

        @pl.when(i == 12)
        def _():
            for d in range(2):
                zs1[d] = part[region_at(2), d].astype(jnp.bfloat16)
                z1(d).start()

        @pl.when(i == 14)
        def _():
            for d in range(2):
                zs2[d, 1 - d] = part[region_at(1 if d == 0 else 3), 1 - d].astype(jnp.bfloat16)
                z2(d, 1 - d).start()

        return carry

    lax.fori_loop(0, RING * RING, turn, 0)

    for d in range(2):
        ys1[d] = dq[y_at(2), d].astype(jnp.bfloat16)
        y1(d).start()
    for d in range(2):
        ys2[d, 1 - d] = dq[y_at(y_step[d]), 1 - d].astype(jnp.bfloat16)
        y2(d, 1 - d).start()
    for d in range(2):
        landed(zr1.at[d], z1_recv.at[d])
        total = part[region_at(1 if d == 0 else 3), d] + zr1[d].astype(jnp.float32)
        zs2[d, d] = total.astype(jnp.bfloat16)
        z2(d, d).start()
    for d in range(2):
        landed(yr1.at[d], y1_recv.at[d])
        total = dq[y_at(y_step[d]), d] + yr1[d].astype(jnp.float32)
        ys2[d, d] = total.astype(jnp.bfloat16)
        y2(d, d).start()

    down = lax.rem(section + sections - 1, sections)

    def out_copy(array, p):
        src, dst, columns = (
            (oq, gq_out, wide(mine)),
            (okv.at[0], gk_out, narrow(mine)),
            (okv.at[1], gv_out, narrow(mine)),
        )[array]
        return remote(
            src.at[pl.ds(pl.multiple_of(p * rows, rows), rows)],
            dst.at[0, :, columns],
            out_send.at[array, p],
            out_recv.at[array],
            {**peer_id(p), "section": down},
        )

    def hand_over(array):
        def one(o, carry):
            out_copy(array, lax.rem(mine + o, PEERS)).start()
            return carry

        lax.fori_loop(0, PEERS, one, 0)

    for b in range(2):
        total = dq[y, b]
        for d in range(2):
            landed(yr2.at[d, b], y2_recv.at[d, b])
            total = total + yr2[d, b].astype(jnp.float32)
        total = total * scale
        for h in range(GROUP):
            oq[b * BLOCK : (b + 1) * BLOCK, h * D : (h + 1) * D] = (
                total[:, h * BLOCK : (h + 1) * BLOCK].T.astype(jnp.bfloat16)
            )
    hand_over(0)
    for i in range(2):
        total = part[region, i]
        for d in range(2):
            landed(zr2.at[d, i], z2_recv.at[d, i])
            total = total + zr2[d, i].astype(jnp.float32)
        okv[i] = (total * scale if i == 0 else total).astype(jnp.bfloat16)
        hand_over(1 + i)

    def end_in(o, carry):
        p = lax.rem(mine + o, PEERS)
        for copy in kv_copies(p) + q_copies(p) + stat_copies(p):
            copy.wait_send()
        return carry

    lax.fori_loop(1, PEERS, end_in, 0)
    for d in range(2):
        for i in range(2):
            ag1(d, i).wait_send()
            z2(d, i).wait_send()
            y2(d, i).wait_send()
        ag2(d).wait_send()
        z1(d).wait_send()
        y1(d).wait_send()
    for o in range(1, RING):
        yt(o).wait_send()
    for p in range(PEERS):
        for d in range(2):
            yq1(p, d).wait_send()
        yq2(p, p % 2).wait_send()

    def end_out(p, carry):
        for array in range(3):
            out_copy(array, p).wait_send()
        return carry

    lax.fori_loop(0, PEERS, end_out, 0)
    for array, out in enumerate((gq_out, gk_out, gv_out)):
        landed(out, out_recv.at[array])


def body(q, k, v, g, lse, delta, lens, table):
    rows = q.shape[1]
    tokens = rows * PEERS
    width = GROUP * D
    pieces = tokens * GROUP
    bf16, f32 = jnp.bfloat16, jnp.float32
    any_space = pl.BlockSpec(memory_space=pl.ANY)
    smem = pl.BlockSpec(memory_space=pltpu.SMEM)
    dma = pltpu.SemaphoreType.DMA
    return pl.pallas_call(
        kernel,
        out_shape=(
            jax.ShapeDtypeStruct(q.shape, bf16),
            jax.ShapeDtypeStruct(k.shape, bf16),
            jax.ShapeDtypeStruct(v.shape, bf16),
        ),
        in_specs=[smem, smem] + [any_space] * 6,
        out_specs=(any_space,) * 3,
        scratch_shapes=[
            pltpu.VMEM((RING, PEERS, 2, rows, width), bf16),
            pltpu.VMEM((RING, pieces, D), bf16),
            pltpu.VMEM((RING, pieces, D), bf16),
            pltpu.VMEM((RING, D, pieces), bf16),
            pltpu.VMEM((RING, D, pieces), bf16),
            pltpu.VMEM((RING, 2, tokens, D), bf16),
            pltpu.VMEM((lse.shape[1], rows), f32),
            pltpu.VMEM((lse.shape[1], rows), f32),
            pltpu.VMEM((PEERS, 8, BLOCK), f32),
            pltpu.VMEM((PEERS, 8, BLOCK), f32),
            pltpu.VMEM((RING, 2, 8, BLOCK), f32),
            pltpu.VMEM((RING, 2, D, width), f32),
            pltpu.VMEM((RING, 2, tokens, D), f32),
            pltpu.VMEM((2, tokens, D), bf16),
            pltpu.VMEM((2, tokens, D), bf16),
            pltpu.VMEM((2, 2, tokens, D), bf16),
            pltpu.VMEM((2, 2, tokens, D), bf16),
            pltpu.VMEM((2, D, width), bf16),
            pltpu.VMEM((2, D, width), bf16),
            pltpu.VMEM((2, 2, D, width), bf16),
            pltpu.VMEM((2, 2, D, width), bf16),
            pltpu.VMEM((tokens, width), bf16),
            pltpu.VMEM((2, tokens, D), bf16),
            dma((2,)),
            dma,
            dma((PEERS,)),
            dma,
            dma((5, PEERS)),
            dma((2, 2)),
            dma((2, 2)),
            dma((2,)),
            dma((2,)),
            dma((2, PEERS)),
            dma((2, PEERS)),
            dma((PEERS,)),
            dma((PEERS,)),
            dma((RING,)),
            dma((RING,)),
            dma((2,)),
            dma((2,)),
            dma((2, 2)),
            dma((2, 2)),
            dma((2,)),
            dma((2,)),
            dma((2, 2)),
            dma((2, 2)),
            dma((3, PEERS)),
            dma((3,)),
        ],
        compiler_params=pltpu.CompilerParams(
            collective_id=0, has_side_effects=True, vmem_limit_bytes=60 * 1024 * 1024
        ),
    )(lens, table, q, k, v, g, lse, delta)


def solution(mesh):
    tokens = P("section", ("ctx", "head"), None)
    totals = P("section", None, ("ctx", "head"))
    return jax.shard_map(
        body,
        mesh=mesh,
        in_specs=(tokens, tokens, tokens, tokens, totals, totals, P("section", None), P()),
        out_specs=(tokens, tokens, tokens),
        check_vma=False,
    )
```

time: 564 us -> 88.2 us (0.16)
  starting transfers between devices: 302 us -> 0 us
  waiting for transfers between devices: 129 us -> 0 us
  Pallas kernels: 0 us -> 82.8 us
  other arithmetic: 47.9 us -> 0 us
  local copies, waits for them, and re-layouts: 32.8 us -> 4.5 us
  loops' own time: 22.3 us -> 0 us
  matrix products: 21.7 us -> 0 us
    ppermute x79 -> x0, starting transfers between devices: 258 us -> none  [shifted(): return lax.ppermute(block, axis, route)]
    ppermute x79 -> x0, waiting for transfers between devices: 98.7 us -> none  [shifted(): return lax.ppermute(block, axis, route)]
    pallas_call x0 -> x1, Pallas kernels: none -> 82.8 us  [body(): pl.pallas_call(kernel, out_shape=(jax.ShapeDtypeStruct(q.shape, bf16), ja...]
    all_to_all x9 -> x0, starting transfers between devices: 44.6 us -> none  [the longest x1 7.62 us: body(): lax.all_to_all(log_sum_exp, 'head', split_axis=1, concat_axis=2, tiled=True)]
    unnamed x7 -> x0, other arithmetic: 42.5 us -> none
    all_to_all x9 -> x0, waiting for transfers between devices: 30.5 us -> none  [the longest x1 6.41 us: body(): lax.all_to_all(query_rows, 'head', split_axis=2, concat_axis=1, tiled=True)]
    another operation x1 -> x0, loops' own time: 22.3 us -> none  [body(): lax.fori_loop(1, ctx_size, query_turn, (query_local, grad_local, lse_loca...]
    dot_general x80 -> x0, matrix products: 21.7 us -> none  [the longest x16 5.46 us: block_terms(): jnp.einsum('ikgd,jkd->kgij', query_heads, key_heads, preferred_element_ty...]
  transfers between devices with their start and end apart: 88 -> 0, of which waited for: 28 -> 0; matrix products, arithmetic and copies ran while one was open for 17% -> 0% of each run, Pallas kernels for 0% -> 0%
where the time goes in v2:
time: 88.2 us; the launch traced here: 87.9 us
  Pallas kernels  82.8 us (94%)
  local copies, waits for them, and re-layouts  4.5 us (5%)
    pallas_call x1, Pallas kernels, body(): pl.pallas_call(kernel, out_shape=(jax.ShapeDtypeStruct(q.shape, bf16), ja...  82.8 us
    unnamed x8, local copies, waits for them, and re-layouts  4.5 us

profile of v2, /device:TPU:1, one launch (start us, length us, event | category | flops | bytes accessed | tf_op | source)
XLA Modules:
  0.0 87.9 jit_solution(11326324574724454552)
XLA Ops:
  0.6 1.4 %copy.11.table = s32[16,2]{1,0:T(8,128)} copy(s32[16,2]{0,1:T(2,128)} %param.15) | data formatting | bytes 256 | tf_op args[7]
  2.0 82.8 %shard_map.103 = (bf16[1,32,3072]{2,1,0:T(8,128)(2,1)}, bf16[1,32,1024]{2,1,0:T(8,128)(2,1)}, bf16[1,32,1024]{2,1,0:T(8,128)(2,1)}) custom-call(s32[1,4]{1,0:T(1,128)} %lens.1, s32[16,2]{1,0:T(8,128)} %copy.11.table, bf16[1,32,3072]{2,1,0:T(8,128)(2,1)} %q_in.1, bf16[1,32,1024]{2,1,0:T(8,128)(2,1)} %k_in.1, bf16[1,32,1024]{2,1,0:T(8,128)(2,1)} %v_in.1, ...), custom_call_target="tpu_custom_call" | custom-call | tf_op jit(solution)/shard_map/pallas_call | solution.py:481
  84.8 0.0 copy-start.1
  84.8 1.6 %copy.15 = bf16[1,32,3072]{2,1,0:T(8,128)(2,1)} copy(bf16[1,32,3072]{2,1,0:T(8,128)(2,1)} %get-tuple-element.6) | data formatting | bytes 393216
  86.4 0.0 copy-done.1
  86.4 0.0 copy-start
  86.4 0.6 copy.16
  87.1 0.2 copy-done
  87.3 0.6 copy.17
Async XLA Ops:
  84.8 1.7 %copy-start.1 = (bf16[1,32,1024]{2,1,0:T(8,128)(2,1)S(1)}, bf16[1,32,1024]{2,1,0:T(8,128)(2,1)}, u32[]{:S(2)}) copy-start(bf16[1,32,1024]{2,1,0:T(8,128)(2,1)} %get-tuple-element.7) | copy-start | bytes 196612
  86.4 0.9 copy-start

commit v3 on v2

--- a/solution.py
+++ b/solution.py
@@ -14,6 +14,7 @@
 PEERS = 8
 RUN = 64
 LOG2E = 1.4426950408889634
+AG_AT = (0, 1)
 MESH = pl.DeviceIdType.MESH
 
 
@@ -60,6 +61,8 @@
     yr2,
     oq,
     okv,
+    lens_held,
+    table_held,
     raw_sem,
     kv_sem,
     q_sem,
@@ -91,12 +94,30 @@
     scale = D ** (-0.5)
     sections = lax.axis_size("section")
     z, place, section = lax.axis_index("ctx"), lax.axis_index("head"), lax.axis_index("section")
+    planes = RING * RING
     region, plane = z // RING, z % RING
     y, x = place // 2, place % 2
     mine = plane * 2 + x
 
-    def peer_id(p):
-        return {"ctx": region * RING + p // 2, "head": y * 2 + p % 2}
+    def piece_plane(at, along_y, u):
+        return lax.rem(at + planes - 2 + along_y % 2 + u, planes)
+
+    def from_id(p):
+        return {"ctx": piece_plane(z, y, p // 2), "head": y * 2 + p % 2}
+
+    def to_plane(k):
+        return lax.rem(z + planes + 2 - y % 2 - k, planes)
+
+    def to_id(k):
+        return {"ctx": to_plane(k // 2), "head": y * 2 + k % 2}
+
+    def head_of(k):
+        return (to_plane(k // 2) % RING) * 2 + k % 2
+
+    def piece_of(k):
+        return (k // 2) * 2 + x
+
+    self_at = (2 - y % 2) * 2 + x
 
     def z_id(d):
         return {"ctx": lax.rem(z + (RING if d == 0 else 3 * RING), RING * RING)}
@@ -121,8 +142,10 @@
 
     raw_lse = pltpu.make_async_copy(lse_in.at[0], lse_raw, raw_sem.at[0])
     raw_delta = pltpu.make_async_copy(delta_in.at[0], delta_raw, raw_sem.at[1])
-    raw_lse.start()
-    raw_delta.start()
+    raw_lens = pltpu.make_async_copy(lens, lens_held, raw_sem.at[2])
+    raw_table = pltpu.make_async_copy(table, table_held, raw_sem.at[3])
+    for copy in (raw_lse, raw_delta, raw_lens, raw_table):
+        copy.start()
 
     barrier = pltpu.get_barrier_semaphore()
 
@@ -130,11 +153,11 @@
         pl.semaphore_signal(barrier, inc=1, device_id=where, device_id_type=MESH)
 
     def greet_peer(o, carry):
-        greet(peer_id(lax.rem(mine + o, PEERS)))
+        greet(from_id(lax.rem(self_at + o, PEERS)))
         return carry
 
     def greet_up(o, carry):
-        greet({**peer_id(lax.rem(mine + o, PEERS)), "section": lax.rem(section + 1, sections)})
+        greet({**to_id(lax.rem(self_at + o, PEERS)), "section": lax.rem(section + 1, sections)})
         return carry
 
     lax.fori_loop(1, PEERS, greet_peer, 0)
@@ -147,45 +170,71 @@
     part[...] = jnp.zeros_like(part)
     dq[...] = jnp.zeros_like(dq)
     stat_out[...] = jnp.zeros_like(stat_out)
-    raw_lse.wait()
-    raw_delta.wait()
+    for copy in (raw_lse, raw_delta, raw_lens, raw_table):
+        copy.wait()
     lanes = lax.broadcasted_iota(jnp.int32, (1, BLOCK), 1)
     per_tile = BLOCK // rows
-    first_lane = rows * (mine % per_tile)
-    own_lanes = (lanes >= first_lane) & (lanes < first_lane + rows)
-    spread_lse = jnp.where(own_lanes, jnp.concatenate([lse_raw[...]] * per_tile, axis=1), 0.0)
-    spread_delta = jnp.where(own_lanes, jnp.concatenate([delta_raw[...]] * per_tile, axis=1), 0.0)
+    wide_lse = jnp.concatenate([lse_raw[...]] * per_tile, axis=1) * LOG2E
+    wide_delta = jnp.concatenate([delta_raw[...]] * per_tile, axis=1)
     for p in range(PEERS):
-        stat_out[p, 0:GROUP] = spread_lse[p * GROUP : (p + 1) * GROUP] * LOG2E
-        stat_out[p, GROUP : 2 * GROUP] = spread_delta[p * GROUP : (p + 1) * GROUP]
+        k = lax.rem(z + 2 - y % 2 - p // 2 + planes, RING)
+        first_lane = rows * ((k % 2) * 2 + x)
+        own_lanes = (lanes >= first_lane) & (lanes < first_lane + rows)
+        of_head = slice(p * GROUP, (p + 1) * GROUP)
+        stat_out[p, 0:GROUP] = jnp.where(own_lanes, wide_lse[of_head], 0.0)
+        stat_out[p, GROUP : 2 * GROUP] = jnp.where(own_lanes, wide_delta[of_head], 0.0)
     pl.semaphore_wait(barrier, 2 * PEERS - 1 + 2 + RING - 1)
 
-    own_rows = pl.ds(pl.multiple_of(mine * rows, rows), rows)
-
-    def narrow(p):
-        return pl.ds(pl.multiple_of(p * D, D), D)
-
-    def wide(p):
-        return pl.ds(pl.multiple_of(p * width, width), width)
-
-    def kv_copies(p):
+    def narrow(h):
+        return pl.ds(pl.multiple_of(h * D, D), D)
+
+    def wide(h):
+        return pl.ds(pl.multiple_of(h * width, width), width)
+
+    def rows_of(p):
+        return pl.ds(pl.multiple_of(p * rows, rows), rows)
+
+    def kv_copies(k):
         return tuple(
-            remote(src.at[0, :, narrow(p)], kv.at[region, i, own_rows], in_send.at[i, p], kv_sem, peer_id(p))
+            remote(
+                src.at[0, :, narrow(head_of(k))],
+                kv.at[region_of(k), i, rows_of(piece_of(k))],
+                in_send.at[i, k],
+                kv_sem,
+                to_id(k),
+            )
             for i, src in enumerate((k_in, v_in))
         )
 
-    def q_copies(p):
+    def region_of(k):
+        return to_plane(k // 2) // RING
+
+    def q_copies(k):
         return tuple(
-            remote(src.at[0, :, wide(p)], qg.at[y, mine, i], in_send.at[2 + i, p], q_sem.at[mine], peer_id(p))
+            remote(
+                src.at[0, :, wide(head_of(k))],
+                qg.at[y, piece_of(k), i],
+                in_send.at[2 + i, k],
+                q_sem.at[piece_of(k)],
+                to_id(k),
+            )
             for i, src in enumerate((q_in, g_in))
         )
 
-    def stat_copies(p):
-        return (remote(stat_out.at[p], stat_in.at[mine], in_send.at[4, p], stat_sem, peer_id(p)),)
+    def stat_copies(k):
+        return (
+            remote(
+                stat_out.at[head_of(k)],
+                stat_in.at[piece_of(k)],
+                in_send.at[4, k],
+                stat_sem,
+                to_id(k),
+            ),
+        )
 
     def to_peers(copies):
         def one(o, carry):
-            for copy in copies(lax.rem(mine + o, PEERS)):
+            for copy in copies(lax.rem(self_at + o, PEERS)):
                 copy.start()
             return carry
 
@@ -193,32 +242,29 @@
 
     to_peers(kv_copies)
     for i, src in enumerate((k_in, v_in)):
-        pltpu.make_async_copy(src.at[0, :, narrow(mine)], kv.at[region, i, own_rows], kv_sem).start()
+        pltpu.make_async_copy(src.at[0, :, narrow(mine)], kv.at[region, i, rows_of(self_at)], kv_sem).start()
     to_peers(stat_copies)
-    pltpu.make_async_copy(stat_out.at[mine], stat_in.at[mine], stat_sem).start()
+    pltpu.make_async_copy(stat_out.at[mine], stat_in.at[self_at], stat_sem).start()
     to_peers(q_copies)
     for i, src in enumerate((q_in, g_in)):
-        pltpu.make_async_copy(src.at[0, :, wide(mine)], qg.at[y, mine, i], q_sem.at[mine]).start()
+        pltpu.make_async_copy(src.at[0, :, wide(mine)], qg.at[y, self_at, i], q_sem.at[self_at]).start()
 
     def region_at(o):
         return lax.rem(region + o, RING)
 
-    def ag1(d, i):
-        return remote(
-            kv.at[region, i], kv.at[region, i], ag1_send.at[d, i], ag1_recv.at[d, i], z_id(d)
-        )
-
-    def ag1_landed(d, i):
-        landed(kv.at[region_at(3 if d == 0 else 1), i], ag1_recv.at[d, i])
-
-    def ag2(d):
-        held = kv.at[region_at(3 if d == 0 else 1), d]
-        return remote(held, held, ag2_send.at[d], ag2_recv.at[d], z_id(d))
-
-    landed(kv.at[region], kv_sem)
-    for i in range(2):
-        for d in range(2):
-            ag1(d, (i + d) % 2).start()
+    def tile_of(c):
+        return pl.ds(c * BLOCK, BLOCK)
+
+    def ag1(d, i, c):
+        held = kv.at[region, i, tile_of(c)]
+        return remote(held, held, ag1_send.at[d, i, c], ag1_recv.at[d, i, c], z_id(d))
+
+    def ag1_landed(d, i, c):
+        landed(kv.at[region_at(3 if d == 0 else 1), i, tile_of(c)], ag1_recv.at[d, i, c])
+
+    def ag2(d, c):
+        held = kv.at[region_at(3 if d == 0 else 1), d, tile_of(c)]
+        return remote(held, held, ag2_send.at[d, c], ag2_recv.at[d, c], z_id(d))
 
     def y_at(o):
         return lax.rem(y + o, RING)
@@ -236,6 +282,29 @@
 
     def yt(o):
         return remote(stat.at[y], stat.at[y], yt_send.at[o], yt_recv.at[o], y_id(o))
+
+    def pass_own(p):
+        landed(qg.at[y, p], q_sem.at[p])
+        for d in range(2):
+            yq1(p, d).start()
+
+    def nearest(odd, j):
+        even_first = (2, 1, 3, 0)[j]
+        return even_first + odd * ((1, 0, 2, 3)[j] - even_first)
+
+    pass_own(self_at)
+    landed(kv.at[region], kv_sem)
+    for i in range(2):
+        for c in range(2):
+            for d in range(2):
+                ag1(d, (i + d) % 2, c).start()
+    for j in range(RING):
+        u = nearest(y % 2, j)
+        if j == 0:
+            pass_own(2 * u + 1 - x)
+        else:
+            pass_own(2 * u)
+            pass_own(2 * u + 1)
 
     landed(stat_in, stat_sem)
     for b in range(2):
@@ -247,13 +316,6 @@
     for o in range(1, RING):
         yt(o).start()
 
-    def pass_own(p, carry):
-        landed(qg.at[y, p], q_sem.at[p])
-        for d in range(2):
-            yq1(p, d).start()
-        return carry
-
-    lax.fori_loop(0, PEERS, pass_own, 0)
 
     def lay_out(at):
         for b in range(2):
@@ -265,22 +327,26 @@
                     stack[at, piece, :] = own
                     turned[at, :, piece] = own.T
 
-    ends = [lens[0, 0]]
+    ends = [lens_held[0, 0]]
     for i in range(1, lens.shape[1]):
-        ends.append(ends[-1] + lens[0, i])
+        ends.append(ends[-1] + lens_held[0, i])
     run_lanes = lanes % RUN
     run_rows = lax.broadcasted_iota(jnp.int32, (RUN, BLOCK), 0)
 
     def visit(yq, r):
         key_start = (y % 2) * RUN
         key_places = jnp.concatenate(
-            [table[r * RING + u, y // 2] * BLOCK + key_start + run_rows for u in range(RING)], axis=0
+            [
+                table_held[y // 2, piece_plane(r * RING + plane, y, u)] * BLOCK + key_start + run_rows
+                for u in range(RING)
+            ],
+            axis=0,
         )
         keys, values = kv[r, 0], kv[r, 1]
         turned_keys = keys.T
         for b in range(2):
             half = slice(b * width, (b + 1) * width)
-            starts_at = [table[region * RING + 2 * b + u, yq // 2] * BLOCK for u in range(2)]
+            starts_at = [table_held[yq // 2, piece_plane(z, yq, 2 * b + u)] * BLOCK for u in range(2)]
             places = jnp.where(lanes < RUN, starts_at[0], starts_at[1]) + (yq % 2) * RUN + run_lanes
             starts = jnp.zeros_like(places)
             for end in ends:
@@ -303,11 +369,19 @@
             part[r, 1] += jnp.dot(weight16, g_stack[yq, half, :], preferred_element_type=jnp.float32)
             dq[yq, b] += jnp.dot(turned_keys, dscore16, preferred_element_type=jnp.float32)
 
-    def z1(d):
-        return remote(zs1.at[d], zr1.at[d], z1_send.at[d], z1_recv.at[d], z_id(d))
-
-    def z2(d, i):
-        return remote(zs2.at[d, i], zr2.at[d, i], z2_send.at[d, i], z2_recv.at[d, i], z_id(d))
+    def z1(d, c):
+        return remote(
+            zs1.at[d, tile_of(c)], zr1.at[d, tile_of(c)], z1_send.at[d, c], z1_recv.at[d, c], z_id(d)
+        )
+
+    def z2(d, i, c):
+        return remote(
+            zs2.at[d, i, tile_of(c)],
+            zr2.at[d, i, tile_of(c)],
+            z2_send.at[d, i, c],
+            z2_recv.at[d, i, c],
+            z_id(d),
+        )
 
     def y1(d):
         return remote(ys1.at[d], yr1.at[d], y1_send.at[d], y1_recv.at[d], y_id(y_step[d]))
@@ -320,14 +394,19 @@
 
         @pl.when(i == 1)
         def _():
-            for d in range(2):
-                ag1_landed(d, d)
-                ag2(d).start()
-            for p in range(PEERS):
-                yq1_landed(p, p % 2)
-                yq2(p, p % 2).start()
-            for d in range(2):
-                ag1_landed(d, 1 - d)
+            for j in range(RING):
+                for d in range(2):
+                    p = 2 * nearest(1 - y % 2, j) + d
+                    yq1_landed(p, d)
+                    yq2(p, d).start()
+                if j in AG_AT:
+                    c = AG_AT.index(j)
+                    for d in range(2):
+                        ag1_landed(d, d, c)
+                        ag2(d, c).start()
+            for c in range(2):
+                for d in range(2):
+                    ag1_landed(d, 1 - d, c)
 
         @pl.when(i == 3)
         def _():
@@ -343,8 +422,9 @@
 
         @pl.when(i == 9)
         def _():
-            for d in range(2):
-                landed(kv.at[region_at(2), d], ag2_recv.at[d])
+            for c in range(2):
+                for d in range(2):
+                    landed(kv.at[region_at(2), d, tile_of(c)], ag2_recv.at[d, c])
 
         @pl.when(i == 12)
         def _():
@@ -352,27 +432,31 @@
                 landed(qg.at[y_at(2), p], yq2_recv.at[p])
             landed(stat.at[y_at(2)], yt_recv.at[2])
 
-        yq, r = y_at(dy), region_at(dr)
-
-        @pl.when((i == 0) | (i == 3) | (i == 6) | (i == 12))
-        def _():
-            lay_out(yq)
-
-        @pl.when((y < 2) | (yq >= 2))
-        def _():
-            visit(yq, r)
-
-        @pl.when(i == 12)
+        @pl.when(i == 13)
         def _():
             for d in range(2):
                 zs1[d] = part[region_at(2), d].astype(jnp.bfloat16)
-                z1(d).start()
-
-        @pl.when(i == 14)
+            for c in range(2):
+                for d in range(2):
+                    z1(d, c).start()
+
+        @pl.when(i == 15)
         def _():
             for d in range(2):
-                zs2[d, 1 - d] = part[region_at(1 if d == 0 else 3), 1 - d].astype(jnp.bfloat16)
-                z2(d, 1 - d).start()
+                side = region_at(1 if d == 0 else 3)
+                zs2[d, 1 - d] = part[side, 1 - d].astype(jnp.bfloat16)
+                for c in range(2):
+                    z2(d, 1 - d, c).start()
+
+        yq, r = y_at(dy), region_at(dr)
+
+        @pl.when((i == 0) | (i == 3) | (i == 6) | (i == 12))
+        def _():
+            lay_out(yq)
+
+        @pl.when((y < 2) | (yq >= 2))
+        def _():
+            visit(yq, r)
 
         return carry
 
@@ -385,15 +469,17 @@
         ys2[d, 1 - d] = dq[y_at(y_step[d]), 1 - d].astype(jnp.bfloat16)
         y2(d, 1 - d).start()
     for d in range(2):
-        landed(zr1.at[d], z1_recv.at[d])
-        total = part[region_at(1 if d == 0 else 3), d] + zr1[d].astype(jnp.float32)
-        zs2[d, d] = total.astype(jnp.bfloat16)
-        z2(d, d).start()
-    for d in range(2):
         landed(yr1.at[d], y1_recv.at[d])
         total = dq[y_at(y_step[d]), d] + yr1[d].astype(jnp.float32)
         ys2[d, d] = total.astype(jnp.bfloat16)
         y2(d, d).start()
+    for c in range(2):
+        for d in range(2):
+            landed(zr1.at[d, tile_of(c)], z1_recv.at[d, c])
+            side = region_at(1 if d == 0 else 3)
+            total = part[side, d, tile_of(c)] + zr1[d, tile_of(c)].astype(jnp.float32)
+            zs2[d, d, tile_of(c)] = total.astype(jnp.bfloat16)
+            z2(d, d, c).start()
 
     down = lax.rem(section + sections - 1, sections)
 
@@ -404,16 +490,16 @@
             (okv.at[1], gv_out, narrow(mine)),
         )[array]
         return remote(
-            src.at[pl.ds(pl.multiple_of(p * rows, rows), rows)],
+            src.at[rows_of(p)],
             dst.at[0, :, columns],
             out_send.at[array, p],
             out_recv.at[array],
-            {**peer_id(p), "section": down},
+            {**from_id(p), "section": down},
         )
 
     def hand_over(array):
         def one(o, carry):
-            out_copy(array, lax.rem(mine + o, PEERS)).start()
+            out_copy(array, lax.rem(self_at + o, PEERS)).start()
             return carry
 
         lax.fori_loop(0, PEERS, one, 0)
@@ -432,25 +518,28 @@
     for i in range(2):
         total = part[region, i]
         for d in range(2):
-            landed(zr2.at[d, i], z2_recv.at[d, i])
+            for c in range(2):
+                landed(zr2.at[d, i, tile_of(c)], z2_recv.at[d, i, c])
             total = total + zr2[d, i].astype(jnp.float32)
         okv[i] = (total * scale if i == 0 else total).astype(jnp.bfloat16)
         hand_over(1 + i)
 
     def end_in(o, carry):
-        p = lax.rem(mine + o, PEERS)
-        for copy in kv_copies(p) + q_copies(p) + stat_copies(p):
+        k = lax.rem(self_at + o, PEERS)
+        for copy in kv_copies(k) + q_copies(k) + stat_copies(k):
             copy.wait_send()
         return carry
 
     lax.fori_loop(1, PEERS, end_in, 0)
     for d in range(2):
         for i in range(2):
-            ag1(d, i).wait_send()
-            z2(d, i).wait_send()
+            for c in range(2):
+                ag1(d, i, c).wait_send()
+                z2(d, i, c).wait_send()
             y2(d, i).wait_send()
-        ag2(d).wait_send()
-        z1(d).wait_send()
+        for c in range(2):
+            ag2(d, c).wait_send()
+            z1(d, c).wait_send()
         y1(d).wait_send()
     for o in range(1, RING):
         yt(o).wait_send()
@@ -469,6 +558,18 @@
         landed(out, out_recv.at[array])
 
 
+def settle(*refs):
+    loads = [pltpu.make_async_copy(refs[i], refs[6 + i], refs[9].at[0, i]) for i in range(3)]
+    stores = [pltpu.make_async_copy(refs[6 + i], refs[3 + i], refs[9].at[1, i]) for i in range(3)]
+    for copy in loads:
+        copy.start()
+    for load, store in zip(loads, stores):
+        load.wait()
+        store.start()
+    for copy in stores:
+        copy.wait()
+
+
 def body(q, k, v, g, lse, delta, lens, table):
     rows = q.shape[1]
     tokens = rows * PEERS
@@ -476,16 +577,15 @@
     pieces = tokens * GROUP
     bf16, f32 = jnp.bfloat16, jnp.float32
     any_space = pl.BlockSpec(memory_space=pl.ANY)
-    smem = pl.BlockSpec(memory_space=pltpu.SMEM)
     dma = pltpu.SemaphoreType.DMA
-    return pl.pallas_call(
+    handed = pl.pallas_call(
         kernel,
         out_shape=(
             jax.ShapeDtypeStruct(q.shape, bf16),
             jax.ShapeDtypeStruct(k.shape, bf16),
             jax.ShapeDtypeStruct(v.shape, bf16),
         ),
-        in_specs=[smem, smem] + [any_space] * 6,
+        in_specs=[any_space] * 8,
         out_specs=(any_space,) * 3,
         scratch_shapes=[
             pltpu.VMEM((RING, PEERS, 2, rows, width), bf16),
@@ -511,25 +611,27 @@
             pltpu.VMEM((2, 2, D, width), bf16),
             pltpu.VMEM((tokens, width), bf16),
             pltpu.VMEM((2, tokens, D), bf16),
-            dma((2,)),
+            pltpu.SMEM(lens.shape, jnp.int32),
+            pltpu.SMEM(table.shape[::-1], jnp.int32),
+            dma((4,)),
             dma,
             dma((PEERS,)),
             dma,
             dma((5, PEERS)),
+            dma((2, 2, 2)),
+            dma((2, 2, 2)),
             dma((2, 2)),
             dma((2, 2)),
-            dma((2,)),
-            dma((2,)),
             dma((2, PEERS)),
             dma((2, PEERS)),
             dma((PEERS,)),
             dma((PEERS,)),
             dma((RING,)),
             dma((RING,)),
-            dma((2,)),
-            dma((2,)),
             dma((2, 2)),
             dma((2, 2)),
+            dma((2, 2, 2)),
+            dma((2, 2, 2)),
             dma((2,)),
             dma((2,)),
             dma((2, 2)),
@@ -540,7 +642,15 @@
         compiler_params=pltpu.CompilerParams(
             collective_id=0, has_side_effects=True, vmem_limit_bytes=60 * 1024 * 1024
         ),
-    )(lens, table, q, k, v, g, lse, delta)
+    )(lens, table.T, q, k, v, g, lse, delta)
+    return pl.pallas_call(
+        settle,
+        out_shape=tuple(jax.ShapeDtypeStruct(out.shape, out.dtype) for out in handed),
+        in_specs=[any_space] * 3,
+        out_specs=(any_space,) * 3,
+        scratch_shapes=[pltpu.VMEM(out.shape, out.dtype) for out in handed] + [dma((2, 3))],
+        compiler_params=pltpu.CompilerParams(vmem_limit_bytes=60 * 1024 * 1024),
+    )(*handed)
 
 
 def solution(mesh):

time: 88.2 us -> 78.8 us (0.89)
  Pallas kernels: 82.8 us -> 77.9 us
  local copies, waits for them, and re-layouts: 4.5 us -> 0 us
    pallas_call x1, Pallas kernels: 82.8 us -> 76.2 us  [body(): pl.pallas_call(kernel, out_shape=(jax.ShapeDtypeStruct(q.shape, bf16), ja...]
    unnamed x8 -> x0, local copies, waits for them, and re-layouts: 4.5 us -> none
    pallas_call x0 -> x1, Pallas kernels: none -> 1.69 us  [body(): pl.pallas_call(settle, out_shape=tuple((jax.ShapeDtypeStruct(out.shape, o...]
where the time goes in v3:
time: 78.8 us; the launch traced here: 78.5 us
  Pallas kernels  77.9 us (99%)
    pallas_call x1, Pallas kernels, body(): pl.pallas_call(kernel, out_shape=(jax.ShapeDtypeStruct(q.shape, bf16), ja...  76.2 us
    pallas_call x1, Pallas kernels, body(): pl.pallas_call(settle, out_shape=tuple((jax.ShapeDtypeStruct(out.shape, o...  1.69 us

profile of v3, /device:TPU:1, one launch (start us, length us, event | category | flops | bytes accessed | tf_op | source)
XLA Modules:
  0.0 78.5 jit_solution(9110106027161680669)
XLA Ops:
  0.6 76.2 %shard_map.103 = (bf16[1,32,3072]{2,1,0:T(8,128)(2,1)}, bf16[1,32,1024]{2,1,0:T(8,128)(2,1)}, bf16[1,32,1024]{2,1,0:T(8,128)(2,1)}) custom-call(s32[1,4]{1,0:T(1,128)} %lens.1, s32[2,16]{1,0:T(2,128)} %bitcast.1, bf16[1,32,3072]{2,1,0:T(8,128)(2,1)} %q_in.1, bf16[1,32,1024]{2,1,0:T(8,128)(2,1)} %k_in.1, bf16[1,32,1024]{2,1,0:T(8,128)(2,1)} %v_in.1, ...), custom_call_target="tpu_custom_call" | custom-call | tf_op jit(solution)/shard_map/pallas_call | solution.py:581
  76.8 1.7 %shard_map.104 = (bf16[1,32,3072]{2,1,0:T(8,128)(2,1)}, bf16[1,32,1024]{2,1,0:T(8,128)(2,1)}, bf16[1,32,1024]{2,1,0:T(8,128)(2,1)}) custom-call(bf16[1,32,3072]{2,1,0:T(8,128)(2,1)} %get-tuple-element.6.refs_0_, bf16[1,32,1024]{2,1,0:T(8,128)(2,1)} %get-tuple-element.7.refs_1_, bf16[1,32,1024]{2,1,0:T(8,128)(2,1)} %get-tuple-element.8.refs_2_), custom_call_target="tpu_custom_call" | custom-call | tf_op jit(solution)/shard_map/pallas_call | solution.py:646

commit v4 on v3

--- a/solution.py
+++ b/solution.py
@@ -18,12 +18,8 @@
 MESH = pl.DeviceIdType.MESH
 
 
-def order_of(i):
-    along_y = (0, 0, 0, 1, 1, 1, 3, 3, 3, 0, 1, 3, 2, 2, 2, 2)
-    along_z = (0, 1, 3, 0, 1, 3, 0, 1, 3, 2, 2, 2, 2, 1, 3, 0)
-    dy = sum(jnp.where(i == k, v, 0) for k, v in enumerate(along_y) if v)
-    dr = sum(jnp.where(i == k, v, 0) for k, v in enumerate(along_z) if v)
-    return dy, dr
+def pick(i, values):
+    return sum(jnp.where(i == k, v, 0) for k, v in enumerate(values) if v)
 
 
 def kernel(
@@ -333,41 +329,43 @@
     run_lanes = lanes % RUN
     run_rows = lax.broadcasted_iota(jnp.int32, (RUN, BLOCK), 0)
 
-    def visit(yq, r):
+    def visit(yq, r, first, count):
+        held = pl.ds(first, count)
         key_start = (y % 2) * RUN
         key_places = jnp.concatenate(
             [
-                table_held[y // 2, piece_plane(r * RING + plane, y, u)] * BLOCK + key_start + run_rows
-                for u in range(RING)
+                table_held[y // 2, piece_plane(r * RING + plane, y, first // RUN + u)] * BLOCK + key_start + run_rows
+                for u in range(count // RUN)
             ],
             axis=0,
         )
-        keys, values = kv[r, 0], kv[r, 1]
+        keys, values = kv[r, 0, held], kv[r, 1, held]
         turned_keys = keys.T
+        scores = jnp.dot(keys, q_turned[yq], preferred_element_type=jnp.float32)
+        grads = jnp.dot(values, g_turned[yq], preferred_element_type=jnp.float32)
+        weights, dscores = [], []
         for b in range(2):
-            half = slice(b * width, (b + 1) * width)
             starts_at = [table_held[yq // 2, piece_plane(z, yq, 2 * b + u)] * BLOCK for u in range(2)]
             places = jnp.where(lanes < RUN, starts_at[0], starts_at[1]) + (yq % 2) * RUN + run_lanes
             starts = jnp.zeros_like(places)
             for end in ends:
                 starts = jnp.where(places >= end, jnp.maximum(starts, end), starts)
             live = (key_places <= places) & (key_places >= starts)
-            scores = jnp.dot(keys, q_turned[yq, :, half], preferred_element_type=jnp.float32)
-            grads = jnp.dot(values, g_turned[yq, :, half], preferred_element_type=jnp.float32)
             totals = stat[yq, b]
-            weights, dscores = [], []
             for h in range(GROUP):
-                at = slice(h * BLOCK, (h + 1) * BLOCK)
+                at = slice((b * GROUP + h) * BLOCK, (b * GROUP + h + 1) * BLOCK)
                 exponent = scores[:, at] * (scale * LOG2E) - totals[h : h + 1, :]
                 weight = jnp.where(live, jnp.exp2(exponent), 0.0)
                 dscore = weight * (grads[:, at] - totals[GROUP + h : GROUP + h + 1, :])
                 weights.append(weight.astype(jnp.bfloat16))
                 dscores.append(dscore.astype(jnp.bfloat16))
-            weight16 = jnp.concatenate(weights, axis=1)
-            dscore16 = jnp.concatenate(dscores, axis=1)
-            part[r, 0] += jnp.dot(dscore16, q_stack[yq, half, :], preferred_element_type=jnp.float32)
-            part[r, 1] += jnp.dot(weight16, g_stack[yq, half, :], preferred_element_type=jnp.float32)
-            dq[yq, b] += jnp.dot(turned_keys, dscore16, preferred_element_type=jnp.float32)
+        weight16 = jnp.concatenate(weights, axis=1)
+        dscore16 = jnp.concatenate(dscores, axis=1)
+        part[r, 0, held] += jnp.dot(dscore16, q_stack[yq], preferred_element_type=jnp.float32)
+        part[r, 1, held] += jnp.dot(weight16, g_stack[yq], preferred_element_type=jnp.float32)
+        dq_all = jnp.dot(turned_keys, dscore16, preferred_element_type=jnp.float32)
+        for b in range(2):
+            dq[yq, b] += dq_all[:, b * width : (b + 1) * width]
 
     def z1(d, c):
         return remote(
@@ -389,8 +387,13 @@
     def y2(d, b):
         return remote(ys2.at[d, b], yr2.at[d, b], y2_send.at[d, b], y2_recv.at[d, b], y_id(y_step[d]))
 
+    def visit_live(yq, r, first, count):
+        @pl.when((y < 2) | (yq >= 2))
+        def _():
+            visit(yq, r, first, count)
+
     def turn(i, carry):
-        dy, dr = order_of(i)
+        yq = y_at(pick(i // 3, (0, 1, 3)))
 
         @pl.when(i == 1)
         def _():
@@ -420,27 +423,50 @@
                 yq1_landed(p, 0)
             landed(stat.at[y_at(3)], yt_recv.at[1])
 
-        @pl.when(i == 9)
+        @pl.when(i % 3 == 0)
         def _():
-            for c in range(2):
+            lay_out(yq)
+
+        visit_live(yq, region_at(pick(i % 3, (0, 1, 3))), 0, 2 * BLOCK)
+        return carry
+
+    lax.fori_loop(0, 9, turn, 0)
+
+    def far_turn(i, carry):
+        for c in range(2):
+
+            @pl.when(i == RING * c)
+            def _():
                 for d in range(2):
                     landed(kv.at[region_at(2), d, tile_of(c)], ag2_recv.at[d, c])
 
-        @pl.when(i == 12)
+        @pl.when(i == 3)
         def _():
             for p in range(PEERS):
                 landed(qg.at[y_at(2), p], yq2_recv.at[p])
             landed(stat.at[y_at(2)], yt_recv.at[2])
-
-        @pl.when(i == 13)
-        def _():
-            for d in range(2):
-                zs1[d] = part[region_at(2), d].astype(jnp.bfloat16)
-            for c in range(2):
+            lay_out(y_at(2))
+
+        visit_live(
+            y_at(pick(i % RING, (0, 1, 3, 2))),
+            region_at(2),
+            pl.multiple_of(i // RING * BLOCK, BLOCK),
+            BLOCK,
+        )
+        for c in range(2):
+
+            @pl.when(i == RING * c + 3)
+            def _():
                 for d in range(2):
+                    zs1[d, tile_of(c)] = part[region_at(2), d, tile_of(c)].astype(jnp.bfloat16)
                     z1(d, c).start()
 
-        @pl.when(i == 15)
+        return carry
+
+    lax.fori_loop(0, 2 * RING, far_turn, 0)
+
+    def last_turn(i, carry):
+        @pl.when(i == 2)
         def _():
             for d in range(2):
                 side = region_at(1 if d == 0 else 3)
@@ -448,19 +474,10 @@
                 for c in range(2):
                     z2(d, 1 - d, c).start()
 
-        yq, r = y_at(dy), region_at(dr)
-
-        @pl.when((i == 0) | (i == 3) | (i == 6) | (i == 12))
-        def _():
-            lay_out(yq)
-
-        @pl.when((y < 2) | (yq >= 2))
-        def _():
-            visit(yq, r)
-
+        visit_live(y_at(2), region_at(pick(i, (1, 3, 0))), 0, 2 * BLOCK)
         return carry
 
-    lax.fori_loop(0, RING * RING, turn, 0)
+    lax.fori_loop(0, 3, last_turn, 0)
 
     for d in range(2):
         ys1[d] = dq[y_at(2), d].astype(jnp.bfloat16)

time: 78.8 us -> 77.2 us (0.980)
  Pallas kernels: 77.9 us -> 75.9 us
    pallas_call x1, Pallas kernels: 76.2 us -> 74.2 us  [body(): pl.pallas_call(kernel, out_shape=(jax.ShapeDtypeStruct(q.shape, bf16), ja...]
where the time goes in v4:
time: 77.2 us; the launch traced here: 76.5 us
  Pallas kernels  75.9 us (98%)
    pallas_call x1, Pallas kernels, body(): pl.pallas_call(kernel, out_shape=(jax.ShapeDtypeStruct(q.shape, bf16), ja...  74.2 us
    pallas_call x1, Pallas kernels, body(): pl.pallas_call(settle, out_shape=tuple((jax.ShapeDtypeStruct(out.shape, o...  1.69 us

profile of v4, /device:TPU:1, one launch (start us, length us, event | category | flops | bytes accessed | tf_op | source)
XLA Modules:
  0.0 76.5 jit_solution(16932553295781676572)
XLA Ops:
  0.6 74.2 %shard_map.103 = (bf16[1,32,3072]{2,1,0:T(8,128)(2,1)}, bf16[1,32,1024]{2,1,0:T(8,128)(2,1)}, bf16[1,32,1024]{2,1,0:T(8,128)(2,1)}) custom-call(s32[1,4]{1,0:T(1,128)} %lens.1, s32[2,16]{1,0:T(2,128)} %bitcast.1, bf16[1,32,3072]{2,1,0:T(8,128)(2,1)} %q_in.1, bf16[1,32,1024]{2,1,0:T(8,128)(2,1)} %k_in.1, bf16[1,32,1024]{2,1,0:T(8,128)(2,1)} %v_in.1, ...), custom_call_target="tpu_custom_call" | custom-call | tf_op jit(solution)/shard_map/pallas_call | solution.py:598
  74.8 1.7 %shard_map.104 = (bf16[1,32,3072]{2,1,0:T(8,128)(2,1)}, bf16[1,32,1024]{2,1,0:T(8,128)(2,1)}, bf16[1,32,1024]{2,1,0:T(8,128)(2,1)}) custom-call(bf16[1,32,3072]{2,1,0:T(8,128)(2,1)} %get-tuple-element.6.refs_0_, bf16[1,32,1024]{2,1,0:T(8,128)(2,1)} %get-tuple-element.7.refs_1_, bf16[1,32,1024]{2,1,0:T(8,128)(2,1)} %get-tuple-element.8.refs_2_), custom_call_target="tpu_custom_call" | custom-call | tf_op jit(solution)/shard_map/pallas_call | solution.py:663

commit v5 on v4

--- a/solution.py
+++ b/solution.py
@@ -393,7 +393,7 @@
             visit(yq, r, first, count)
 
     def turn(i, carry):
-        yq = y_at(pick(i // 3, (0, 1, 3)))
+        yq = y_at(pick(i % 3, (0, 1, 3)))
 
         @pl.when(i == 1)
         def _():
@@ -407,27 +407,27 @@
                     for d in range(2):
                         ag1_landed(d, d, c)
                         ag2(d, c).start()
-            for c in range(2):
-                for d in range(2):
-                    ag1_landed(d, 1 - d, c)
-
-        @pl.when(i == 3)
-        def _():
             for p in range(0, PEERS, 2):
                 yq1_landed(p, 1)
             landed(stat.at[y_at(1)], yt_recv.at[3])
 
-        @pl.when(i == 6)
+        @pl.when(i == 2)
         def _():
             for p in range(1, PEERS, 2):
                 yq1_landed(p, 0)
             landed(stat.at[y_at(3)], yt_recv.at[1])
 
-        @pl.when(i % 3 == 0)
+        @pl.when(i == 3)
+        def _():
+            for c in range(2):
+                for d in range(2):
+                    ag1_landed(d, 1 - d, c)
+
+        @pl.when(i < 3)
         def _():
             lay_out(yq)
 
-        visit_live(yq, region_at(pick(i % 3, (0, 1, 3))), 0, 2 * BLOCK)
+        visit_live(yq, region_at(pick(i // 3, (0, 1, 3))), 0, 2 * BLOCK)
         return carry
 
     lax.fori_loop(0, 9, turn, 0)

time: 77.2 us -> 76.4 us (0.990)
  no operation moved by 1% of the time
where the time goes in v5:
time: 76.4 us; the launch traced here: 76.1 us
  Pallas kernels  75.5 us (99%)
    pallas_call x1, Pallas kernels, body(): pl.pallas_call(kernel, out_shape=(jax.ShapeDtypeStruct(q.shape, bf16), ja...  73.8 us
    pallas_call x1, Pallas kernels, body(): pl.pallas_call(settle, out_shape=tuple((jax.ShapeDtypeStruct(out.shape, o...  1.69 us

profile of v5, /device:TPU:1, one launch (start us, length us, event | category | flops | bytes accessed | tf_op | source)
XLA Modules:
  0.0 76.1 jit_solution(7885830160605533648)
XLA Ops:
  0.6 73.8 %shard_map.103 = (bf16[1,32,3072]{2,1,0:T(8,128)(2,1)}, bf16[1,32,1024]{2,1,0:T(8,128)(2,1)}, bf16[1,32,1024]{2,1,0:T(8,128)(2,1)}) custom-call(s32[1,4]{1,0:T(1,128)} %lens.1, s32[2,16]{1,0:T(2,128)} %bitcast.1, bf16[1,32,3072]{2,1,0:T(8,128)(2,1)} %q_in.1, bf16[1,32,1024]{2,1,0:T(8,128)(2,1)} %k_in.1, bf16[1,32,1024]{2,1,0:T(8,128)(2,1)} %v_in.1, ...), custom_call_target="tpu_custom_call" | custom-call | tf_op jit(solution)/shard_map/pallas_call | solution.py:598
  74.4 1.7 %shard_map.104 = (bf16[1,32,3072]{2,1,0:T(8,128)(2,1)}, bf16[1,32,1024]{2,1,0:T(8,128)(2,1)}, bf16[1,32,1024]{2,1,0:T(8,128)(2,1)}) custom-call(bf16[1,32,3072]{2,1,0:T(8,128)(2,1)} %get-tuple-element.6.refs_0_, bf16[1,32,1024]{2,1,0:T(8,128)(2,1)} %get-tuple-element.7.refs_1_, bf16[1,32,1024]{2,1,0:T(8,128)(2,1)} %get-tuple-element.8.refs_2_), custom_call_target="tpu_custom_call" | custom-call | tf_op jit(solution)/shard_map/pallas_call | solution.py:663

commit v6 on v5

--- a/solution.py
+++ b/solution.py
@@ -466,9 +466,10 @@
     lax.fori_loop(0, 2 * RING, far_turn, 0)
 
     def last_turn(i, carry):
-        @pl.when(i == 2)
-        def _():
-            for d in range(2):
+        for d in range(2):
+
+            @pl.when(i == 1 + d)
+            def _(d=d):
                 side = region_at(1 if d == 0 else 3)
                 zs2[d, 1 - d] = part[side, 1 - d].astype(jnp.bfloat16)
                 for c in range(2):

time: 76.4 us -> 76.8 us (level)
  no operation moved by 1% of the time
where the time goes in v6:
time: 76.8 us; the launch traced here: 76.6 us
  Pallas kernels  75.9 us (99%)
    pallas_call x1, Pallas kernels, body(): pl.pallas_call(kernel, out_shape=(jax.ShapeDtypeStruct(q.shape, bf16), ja...  74.2 us
    pallas_call x1, Pallas kernels, body(): pl.pallas_call(settle, out_shape=tuple((jax.ShapeDtypeStruct(out.shape, o...  1.69 us

profile of v6, /device:TPU:1, one launch (start us, length us, event | category | flops | bytes accessed | tf_op | source)
XLA Modules:
  0.0 76.6 jit_solution(12078381497963960709)
XLA Ops:
  0.6 74.2 %shard_map.103 = (bf16[1,32,3072]{2,1,0:T(8,128)(2,1)}, bf16[1,32,1024]{2,1,0:T(8,128)(2,1)}, bf16[1,32,1024]{2,1,0:T(8,128)(2,1)}) custom-call(s32[1,4]{1,0:T(1,128)} %lens.1, s32[2,16]{1,0:T(2,128)} %bitcast.1, bf16[1,32,3072]{2,1,0:T(8,128)(2,1)} %q_in.1, bf16[1,32,1024]{2,1,0:T(8,128)(2,1)} %k_in.1, bf16[1,32,1024]{2,1,0:T(8,128)(2,1)} %v_in.1, ...), custom_call_target="tpu_custom_call" | custom-call | tf_op jit(solution)/shard_map/pallas_call | solution.py:599
  74.9 1.7 %shard_map.104 = (bf16[1,32,3072]{2,1,0:T(8,128)(2,1)}, bf16[1,32,1024]{2,1,0:T(8,128)(2,1)}, bf16[1,32,1024]{2,1,0:T(8,128)(2,1)}) custom-call(bf16[1,32,3072]{2,1,0:T(8,128)(2,1)} %get-tuple-element.6.refs_0_, bf16[1,32,1024]{2,1,0:T(8,128)(2,1)} %get-tuple-element.7.refs_1_, bf16[1,32,1024]{2,1,0:T(8,128)(2,1)} %get-tuple-element.8.refs_2_), custom_call_target="tpu_custom_call" | custom-call | tf_op jit(solution)/shard_map/pallas_call | solution.py:664
